TPU v7x, 256 devices: a whole 4x4x8 slice. The times are simulated.
256 devices in a mesh: shot: 16 (over z_hi, x), rcv: 16 (over z_lo, y, core).
Axes of the slice: x: 4, y: 4, z: 8 (z_hi: 4, z_lo: 2; z = z_hi * 2 + z_lo), core: 2. Of those that a mesh axis runs over, the one named last changes fastest.
Arguments:
- spectra: bfloat16 [16, 16384, 2, 1024], P('rcv', 'shot'), may hold values from -6 to 6
- shot_grid: int32 [2, 16384], P(None, 'shot'), may hold values from 0 to 127
- ray_table: int32 [2, 512], replicated, may hold values from -16 to 15
- receiver_grid: int32 [2, 1024], replicated, may hold values from 0 to 63
Outputs:
- encoded: bfloat16 [512, 16, 2, 1024], P(('shot', 'rcv'))
All inputs are finite; a program needn't handle non-finite values.
Results may differ from a plain program's by a relative error of at most 0.0042.
Values may be sent and summed in bfloat16 or wider, within the bound.
No kernel may reach another device: no remote copies, remote signals or barrier semaphores. Data moves between devices by JAX's collectives and lax.ppermute only.
A program may use at most 64 MiB of HBM per device.

v0:
```python
import math

import jax
import jax.numpy as jnp
from jax import lax
from jax.sharding import PartitionSpec as P

base_index = 5
modulus = 1024


def on_device(spectra, shot_grid, ray_table, receiver_grid):
    freq_local = spectra.shape[0]
    shot_local = spectra.shape[1]
    width = spectra.shape[3]
    rays_all = ray_table.shape[1]
    shot_groups = lax.axis_size("shot")
    rays_share = rays_all // shot_groups
    step_angle = 2.0 * math.pi / modulus
    gscale = 1.0 / math.sqrt(shot_local * shot_groups)
    first_wave = base_index + lax.axis_index("rcv") * freq_local
    shot_index = lax.axis_index("shot")
    local_data = spectra.reshape(freq_local, shot_local, 2 * width)
    offset = 0
    wave = first_wave + offset
    counted = (
        wave
        * (
            ray_table[0][:, None] * shot_grid[0][None, :]
            + ray_table[1][:, None] * shot_grid[1][None, :]
        )
        % modulus
    )
    angle = counted.astype(jnp.float32) * step_angle
    phases = jnp.concatenate([jnp.cos(angle), jnp.sin(angle)], 0).astype(jnp.bfloat16)
    product = jnp.dot(phases, local_data[offset], preferred_element_type=jnp.float32)
    real_part = product[:rays_all, :width] + product[rays_all:, width:]
    imag_part = product[:rays_all, width:] - product[rays_all:, :width]
    pieces = [jnp.stack([real_part, imag_part], 1)]
    summed = lax.psum(jnp.stack(pieces, 1), "shot")
    owned = lax.dynamic_slice_in_dim(summed, shot_index * rays_share, rays_share, 0)
    own_rays = lax.dynamic_slice_in_dim(ray_table, shot_index * rays_share, rays_share, 1)
    offset = 0
    wave = first_wave + offset
    counted = (
        wave
        * (
            own_rays[0][:, None] * receiver_grid[0][None, :]
            + own_rays[1][:, None] * receiver_grid[1][None, :]
        )
        % modulus
    )
    angle = counted.astype(jnp.float32) * step_angle
    cosine = jnp.cos(angle)
    sine = jnp.sin(angle)
    real_part = owned[:, offset, 0, :]
    imag_part = owned[:, offset, 1, :]
    out_real = gscale * (real_part * cosine - imag_part * sine)
    out_imag = gscale * (real_part * sine + imag_part * cosine)
    rotated_list = [jnp.stack([out_real, out_imag], 1)]
    rotated = jnp.stack(rotated_list, 1).astype(jnp.bfloat16)
    return lax.all_to_all(rotated, "rcv", split_axis=0, concat_axis=1, tiled=True)


def solution(mesh):
    in_specs = (P("rcv", "shot", None, None), P(None, "shot"), P(), P())
    out_specs = P(("shot", "rcv"), None, None, None)
    return jax.shard_map(
        on_device, mesh=mesh, in_specs=in_specs, out_specs=out_specs, check_vma=False
    )
```

profile of v0, /device:TPU:1, one launch (start us, length us, event | category | flops | bytes accessed | tf_op | source)
XLA Modules:
  0.0 279.2 jit_solution(697881233819256686)
XLA Ops:
  6.5 0.0 all-reduce.2.cloned.1.call-start
  6.5 0.8 fusion.16
  7.3 0.8 fusion.17
  8.1 5.6 %copy.8 = bf16[128,8,2,1024]{3,1,2,0:T(8,128)(2,1)} copy(bf16[128,8,2,1024]{3,2,1,0:T(2,128)(2,1)} %bitcast.26) | data formatting | bytes 8388608
  13.6 9.2 %cosine_convert_fusion = (bf16[512,1024]{1,0:T(8,128)(2,1)S(1)}, bf16[512,1024]{1,0:T(8,128)(2,1)S(1)}) fusion(s32[1024]{0:T(1024)S(1)} %bitcast.32, s32[512]{0:T(512)S(1)} %bitcast.34, s32[1024]{0:T(1024)S(1)} %bitcast.31, s32[512]{0:T(512)S(1)} %bitcast.33, s32[]{:T(128)S(6)} %add_shard_map.3), kind=kLoop, calls=%fused_computation.16 | loop fusion | flops 9961472 | bytes 2109444 | tf_op jit(solution)/shard_map/convert.2
  22.9 6.3 %fusion.5 = f32[1024,2048]{1,0:T(8,128)S(1)} fusion(bf16[1024,2048]{1,0:T(8,128)(2,1)} %bitcast.27, bf16[512,1024]{1,0:T(8,128)(2,1)S(1)} %get-tuple-element.10, bf16[512,1024]{1,0:T(8,128)(2,1)S(1)} %get-tuple-element.9), kind=kOutput, calls=%fused_computation.11 | convolution fusion | flops 4299161600 | bytes 14680064 | tf_op jit(solution)/shard_map/dot_general | solution.py:36
  29.2 1.4 fusion.4
  30.5 2.3 maximum_bitcast_fusion
  32.8 0.0 copy-start
  32.8 0.0 all-reduce.2.cloned.1.call-update
  32.9 0.8 constant_dynamic-slice_fusion
  33.6 0.0 copy-done
  33.6 219.5 %all-reduce.2.cloned.1.call-done = f32[512,1,2,1024]{3,0,2,1:T(8,128)} async-done(((f32[512,1,2,1024]{3,0,2,1:T(8,128)}), f32[512,1,2,1024]{3,0,2,1:T(8,128)}) %all-reduce.2.cloned.1.call-update) | async-done | bytes 4194320 | tf_op jit(solution)/shard_map/psum | solution.py:40
  253.1 1.6 multiply_convert_fusion.1
  254.8 0.1 copy.6
  254.9 16.7 %all_to_all.18 = bf16[32,1,2,1024]{3,2,1,0:T(2,128)(2,1)S(1)} all-to-all(bf16[32,1,2,1024]{3,2,1,0:T(2,128)(2,1)S(1)} %copy.6), channel_id=1, replica_groups=mesh['shot'=16,'rcv'=16] {'rcv'}, dimensions={0} | all-to-all | bytes 262144 | tf_op jit(solution)/shard_map/all_to_all | solution.py:62
  271.6 0.7 copy.10
  (3 shorter events, 0.0 us)
Async XLA Ops:
  6.5 246.6 %all-reduce.2.cloned.1.call-start = ((), (), s32[]{:S(2)}) async-start(), calls=%async_computation.1 | async-start | bytes 8388608 | tf_op jit(solution)/shard_map/psum | solution.py:40
  32.8 0.8 copy-start
Sparse Core Ops, SparseCore 0:
  33.0 220.1 all-reduce.1
where the time goes:
time: 279 us
  waiting for transfers between devices  220 us (79%)
  blocking collectives  16.7 us (6%)
  other arithmetic  14.5 us (5%)
  between operations  13.4 us (5%)
  local copies, waits for them, and re-layouts  8.76 us (3%)
  matrix products  6.29 us (2%)
    psum x1, waiting for transfers between devices, on_device(): summed = lax.psum(jnp.stack(pieces, 1), 'shot')  219 us
    all_to_all x1, blocking collectives, on_device(): lax.all_to_all(rotated, 'rcv', split_axis=0, concat_axis=1, tiled=True)  16.7 us
    another operation x2, other arithmetic  10.8 us
    dot_general x1, matrix products, on_device(): jnp.dot(phases, local_data[offset], preferred_element_type=jnp.float32)  6.29 us
  transfers between devices with their start and end apart: 1, of which 1 were waited for; matrix products, arithmetic and copies ran while one was open for 0% of the time, Pallas kernels for 0%

commit v1 on v0

v1 whole, which is shorter than its diff:
```python
import functools
import math

import jax
import jax.numpy as jnp
import numpy as np
from jax import lax
from jax.experimental import pallas as pl
from jax.experimental.pallas import tpu as pltpu
from jax.sharding import PartitionSpec as P

BASE = 5
MODULUS = 1024
ZH, XS, ZL, YS, CORES = 4, 4, 2, 4, 2
SHOT, RCV = ZH * XS, ZL * YS * CORES
RAYS, WIDTH, LOCAL = 512, 1024, 1024
SHARE = RAYS // SHOT
XFIRST = 24
ZFIRST = SHARE - XFIRST
VMEM = pl.BlockSpec(memory_space=pltpu.VMEM)
SMEM = pl.BlockSpec(memory_space=pltpu.SMEM)
ANY = pl.BlockSpec(memory_space=pl.ANY)


def fitted(fn, degree):
    points = 0.125 * (1 + np.cos(np.pi * (np.arange(400) + 0.5) / 400))
    series = np.polynomial.chebyshev.Chebyshev.fit(points, fn(np.sqrt(points)), degree, domain=[0, 0.25])
    return [float(a) for a in series.convert(kind=np.polynomial.Polynomial).coef]


COS = fitted(lambda f: np.cos(2 * np.pi * f), 5)
SIN = fitted(lambda f: np.sin(2 * np.pi * f) / f, 5)


def horner(coefs, v):
    total = v * coefs[-1] + coefs[-2]
    for a in coefs[-3::-1]:
        total = total * v + a
    return total


def cos_sin(turns):
    f = turns - jnp.round(turns)
    v = f * f
    return horner(COS, v), f * horner(SIN, v)


def place(index):
    shot, rcv = index // RCV, index % RCV
    return shot // XS, shot % XS, rcv // (YS * CORES), rcv // CORES % YS, rcv % CORES


def joined(zh, x, zl, y, core):
    return ((zh % ZH) * XS + x % XS) * RCV + (zl * YS + y) * CORES + core


def pairs(axis, steps):
    out = []
    for index in range(SHOT * RCV):
        zh, x, zl, y, core = place(index)
        step = steps[core]
        out.append((index, joined(zh + step, x, zl, y, core) if axis == "z" else joined(zh, x + step, zl, y, core)))
    return out


def send(value, axis, steps):
    return lax.ppermute(value, ("shot", "rcv"), pairs(axis, steps))


STEPS = ((2, 2), (1, 3), (3, 1))


def picked(ray, row_of_lane, rows):
    chosen = (lax.broadcasted_iota(jnp.int32, (rows, ray.shape[1]), 0) == row_of_lane).astype(jnp.bfloat16)
    return lax.dot_general(chosen, ray, (((1,), (1,)), ((), ())), preferred_element_type=jnp.float32)


def phase_rows(groups, info_ref, ray_ref, shot_ref, lhs):
    ray = ray_ref[...].astype(jnp.float32).astype(jnp.bfloat16)
    lane = lax.broadcasted_iota(jnp.int32, (1, RAYS), 1)
    zh_of, x_of, q_of = lane // (RAYS // ZH), lane // SHARE % XS, lane % SHARE
    odd = (lax.broadcasted_iota(jnp.int32, (1, 256), 1) % 2).astype(jnp.float32) * 0.25
    base = 0
    for slot, (axis, low, m) in enumerate(groups):
        target = info_ref[slot]
        along, other = (x_of, zh_of) if axis == "x" else (zh_of, x_of)
        mine = (along == target) & (q_of >= low) & (q_of < low + m)
        p = picked(ray, jnp.where(mine, other * m + q_of - low, -1), 4 * m)

        def step(k, carry, p=p, base=base, m=m):
            at = pl.ds(pl.multiple_of(k * 256, 256), 256)
            g0, g1 = shot_ref[0:1, at], shot_ref[1:2, at]
            for i in range(4):
                rays = p[i * m : (i + 1) * m]
                c, s = cos_sin(rays[:, 0:1] * g0 + rays[:, 1:2] * g1 - odd)
                lhs[base + 2 * m * i : base + 2 * m * (i + 1), at] = jnp.concatenate([c, -s], 0).astype(jnp.bfloat16)
            return carry

        lax.fori_loop(0, 2 * LOCAL // 256, step, 0)
        base += 8 * m


def products(groups, lhs, data_ref, outs):
    for i in range(WIDTH // 256):
        at = slice(i * 256, (i + 1) * 256)
        block = data_ref[:, at]
        base = 0
        for (axis, low, m), out in zip(groups, outs):
            r = jnp.dot(lhs[base : base + 8 * m], block, preferred_element_type=jnp.float32)
            out[:, at] = r.astype(out.dtype)
            base += 8 * m


def first_kernel(groups, info_ref, ray_ref, shot_ref, x_ref, *refs):
    outs, (data_ref, lhs, buf, sems) = refs[: len(groups)], refs[len(groups) :]
    part = LOCAL // 8
    copies = []
    for i in range(8):
        at = pl.ds(i * part, part)
        copies.append(pltpu.make_async_copy(x_ref.at[at], buf.at[at], sems.at[i]))
        copies[-1].start()
    phase_rows(groups, info_ref, ray_ref, shot_ref, lhs)
    for i in range(8):
        copies[i].wait()
        for s in range(i * part, (i + 1) * part, 8):
            data_ref[2 * s : 2 * s + 16] = buf[s : s + 8].reshape(16, WIDTH)
    products(groups, lhs, data_ref, outs)


def later_kernel(groups, info_ref, ray_ref, shot_ref, data_ref, *refs):
    outs, (lhs,) = refs[: len(groups)], refs[len(groups) :]
    phase_rows(groups, info_ref, ray_ref, shot_ref, lhs)
    products(groups, lhs, data_ref, outs)


def encode(groups, info, ray_table, shots, x, dtype, first):
    rows = sum(8 * m for _, _, m in groups)
    shapes = [jax.ShapeDtypeStruct((8 * m, WIDTH), dtype) for _, _, m in groups]
    scratch = [pltpu.VMEM((rows, 2 * LOCAL), jnp.bfloat16)]
    if first:
        shapes.append(jax.ShapeDtypeStruct((2 * LOCAL, WIDTH), jnp.bfloat16))
        scratch += [pltpu.VMEM((LOCAL, 2, WIDTH), jnp.bfloat16), pltpu.SemaphoreType.DMA((8,))]
    return pl.pallas_call(
        functools.partial(first_kernel if first else later_kernel, groups),
        out_shape=shapes,
        in_specs=[SMEM, VMEM, VMEM, ANY if first else VMEM],
        out_specs=[VMEM] * len(shapes),
        scratch_shapes=scratch,
        compiler_params=pltpu.CompilerParams(vmem_limit_bytes=28 * 2**20),
        cost_estimate=pl.CostEstimate(flops=2 * rows * 2 * LOCAL * WIDTH, bytes_accessed=8 * 2**20, transcendentals=0),
        name="encode_first" if first else "encode_later",
    )(info, ray_table, shots, x)


def merge_kernel(n_in, unit, info_ref, *refs):
    ins, outs = refs[:n_in], refs[n_in:]
    for k, out in enumerate(outs):
        at = pl.ds(pl.multiple_of(info_ref[k] * unit, 16), unit)
        total = ins[0][at, :].astype(jnp.float32)
        for piece in ins[1:]:
            total = total + piece[at, :].astype(jnp.float32)
        out[...] = total.astype(out.dtype)


def merge(info, own, received):
    unit = own.shape[0] // 4
    ins = [own, *received]
    return pl.pallas_call(
        functools.partial(merge_kernel, len(ins), unit),
        out_shape=[jax.ShapeDtypeStruct((unit, WIDTH), d) for d in (jnp.bfloat16,) * 3 + (jnp.float32,)],
        in_specs=[SMEM] + [VMEM] * len(ins),
        out_specs=[VMEM] * 4,
        name="merge",
    )(info, *ins)


def last_kernel(scale, info_ref, ray_ref, rcv_ref, *refs):
    ins, out = refs[:-1], refs[-1]
    target, turn = info_ref[0], info_ref[1].astype(jnp.float32) / MODULUS
    ray = ray_ref[...].astype(jnp.float32).astype(jnp.bfloat16)
    lane = lax.broadcasted_iota(jnp.int32, (1, RAYS), 1)
    p = picked(ray, lane - target * SHARE, SHARE)
    for i in range(WIDTH // 256):
        at = slice(i * 256, (i + 1) * 256)
        grid = rcv_ref[:, at].astype(jnp.float32)
        c, s = cos_sin((p[:, 0:1] * grid[0:1] + p[:, 1:2] * grid[1:2]) * turn)
        parts = []
        for some in (ins[:4], ins[4:]):
            total = some[0][:, at]
            for piece in some[1:]:
                total = total + piece[:, at].astype(jnp.float32)
            parts.append(total)
        re = jnp.concatenate([parts[0][:XFIRST], parts[1][:ZFIRST]], 0)
        im = jnp.concatenate([parts[0][XFIRST:], parts[1][ZFIRST:]], 0)
        out[0, :, at] = (scale * (re * c - im * s)).astype(jnp.bfloat16)
        out[1, :, at] = (scale * (re * s + im * c)).astype(jnp.bfloat16)


def on_device(spectra, shot_grid, ray_table, receiver_grid):
    shot, rcv = lax.axis_index("shot"), lax.axis_index("rcv")
    zh, x, core = shot // XS, shot % XS, rcv % CORES
    wave = BASE + rcv
    scale = 1.0 / math.sqrt(LOCAL * SHOT)
    shots = jnp.repeat(shot_grid, 2, axis=1).astype(jnp.float32) * (wave.astype(jnp.float32) / MODULUS)

    def goal(at, steps):
        return (at + jnp.where(core == 0, steps[0], steps[1])) % 4

    xs = [goal(x, s) for s in STEPS] + [x]
    zs = [goal(zh, s) for s in STEPS] + [zh]
    px, qz = ("x", 0, XFIRST), ("z", XFIRST, ZFIRST)
    data = spectra.reshape(LOCAL, 2, WIDTH)

    def info(*values):
        return jnp.stack([v.astype(jnp.int32) for v in values])

    p0, q0, data = encode([px, qz], info(xs[0], zs[0]), ray_table, shots, data, jnp.bfloat16, True)
    from_x = [send(p0, "x", STEPS[0])]
    from_z = [send(q0, "z", STEPS[0])]
    p1, p2, q1, q2 = encode([px, px, qz, qz], info(xs[1], xs[2], zs[1], zs[2]), ray_table, shots, data, jnp.bfloat16, False)
    from_x += [send(p1, "x", STEPS[1]), send(p2, "x", STEPS[2])]
    from_z += [send(q1, "z", STEPS[1]), send(q2, "z", STEPS[2])]
    p3, q3 = encode([px, qz], info(xs[3], zs[3]), ray_table, shots, data, jnp.float32, False)
    half = merge(info(*zs), p3, from_x)
    other = merge(info(*xs), q3, from_z)
    ins = [half[3]] + [send(half[k], "z", STEPS[k]) for k in range(3)]
    ins += [other[3]] + [send(other[k], "x", STEPS[k]) for k in range(3)]
    turned = pl.pallas_call(
        functools.partial(last_kernel, scale),
        out_shape=jax.ShapeDtypeStruct((2, SHARE, WIDTH), jnp.bfloat16),
        in_specs=[SMEM] + [VMEM] * 10,
        out_specs=VMEM,
        name="last",
    )(info(shot, wave), ray_table, receiver_grid, *ins)
    mine = jnp.transpose(turned, (1, 0, 2)).reshape(SHARE, 1, 2, WIDTH)
    return lax.all_to_all(mine, "rcv", split_axis=0, concat_axis=1, tiled=True)


def solution(mesh):
    in_specs = (P("rcv", "shot", None, None), P(None, "shot"), P(), P())
    out_specs = P(("shot", "rcv"), None, None, None)
    return jax.shard_map(on_device, mesh=mesh, in_specs=in_specs, out_specs=out_specs, check_vma=False)
```

time: 279 us -> 87.8 us (0.31)
  waiting for transfers between devices: 220 us -> 9.25 us
  Pallas kernels: 0 us -> 25.9 us
  starting transfers between devices: 0.01 us -> 22.5 us
  between operations: 13.4 us -> 0.18 us
  other arithmetic: 14.5 us -> 2.92 us
  matrix products: 6.29 us -> 0 us
  local copies, waits for them, and re-layouts: 8.76 us -> 13.6 us
  blocking collectives: 16.7 us -> 13.1 us
    psum x1 -> x0, waiting for transfers between devices: 219 us -> none  [on_device(): summed = lax.psum(jnp.stack(pieces, 1), 'shot')]
    pallas_call x0 -> x6, Pallas kernels: none -> 25.9 us  [the longest x3 19.6 us: encode(): pl.pallas_call(functools.partial(first_kernel if first else later_kernel,...]
    ppermute x0 -> x12, starting transfers between devices: none -> 22.5 us  [send(): return lax.ppermute(value, ('shot', 'rcv'), pairs(axis, steps))]
    another operation x5 -> x6, other arithmetic: 14.5 us -> 2.2 us  [info(): return jnp.stack([v.astype(jnp.int32) for v in values])]
    ppermute x0 -> x12, waiting for transfers between devices: none -> 9.25 us  [send(): return lax.ppermute(value, ('shot', 'rcv'), pairs(axis, steps))]
    dot_general x1 -> x0, matrix products: 6.29 us -> none  [on_device(): jnp.dot(phases, local_data[offset], preferred_element_type=jnp.float32)]
    unnamed x3 -> x38, local copies, waits for them, and re-layouts: 5.56 us -> 10.9 us
    all_to_all x1, blocking collectives: 16.7 us -> 13.1 us  [on_device(): return lax.all_to_all(mine, 'rcv', split_axis=0, concat_axis=1, tiled=True)]
  transfers between devices with their start and end apart: 1 -> 12, of which waited for: 1 -> 4; matrix products, arithmetic and copies ran while one was open for 0% -> 2% of each run, Pallas kernels for 0% -> 21%
where the time goes in v1:
time: 87.8 us; the launch traced here: 87.5 us
  Pallas kernels  25.9 us (29%)
  starting transfers between devices  22.5 us (26%)
  local copies, waits for them, and re-layouts  13.6 us (15%)
  blocking collectives  13.1 us (15%)
  waiting for transfers between devices  9.25 us (11%)
  other arithmetic  2.92 us (3%)
    ppermute x12, starting transfers between devices, send(): return lax.ppermute(value, ('shot', 'rcv'), pairs(axis, steps))  22.5 us
    pallas_call x3, Pallas kernels, encode(): pl.pallas_call(functools.partial(first_kernel if first else later_kernel,...  19.6 us
    all_to_all x1, blocking collectives, on_device(): return lax.all_to_all(mine, 'rcv', split_axis=0, concat_axis=1, tiled=True)  13.1 us
    unnamed x38, local copies, waits for them, and re-layouts  10.9 us
    ppermute x12, waiting for transfers between devices, send(): return lax.ppermute(value, ('shot', 'rcv'), pairs(axis, steps))  9.25 us
    pallas_call x2, Pallas kernels, merge(): pl.pallas_call(functools.partial(merge_kernel, len(ins), unit), out_shape...  4.15 us
    another operation x6, other arithmetic, info(): return jnp.stack([v.astype(jnp.int32) for v in values])  2.2 us
    pallas_call x1, Pallas kernels, on_device(): pl.pallas_call(functools.partial(last_kernel, scale), out_shape=jax.Shape...  2.18 us
  transfers between devices with their start and end apart: 12, of which 4 were waited for; matrix products, arithmetic and copies ran while one was open for 2% of the time, Pallas kernels for 21%

profile of v1, /device:TPU:1, one launch (start us, length us, event | category | flops | bytes accessed | tf_op | source)
XLA Modules:
  0.0 87.5 jit_solution(588130523684347523)
XLA Ops:
  0.0 0.7 convert_multiply_fusion
  0.7 0.3 broadcast_in_dim.3
  1.0 0.6 mul.10.shot_ref
  1.7 0.1 pad_add_fusion.3.info_ref
  1.7 2.2 %copy-done = bf16[1,1024,2,1024]{3,2,1,0:T(2,128)(2,1)S(1)} copy-done((bf16[1,1024,2,1024]{3,2,1,0:T(2,128)(2,1)S(1)}, bf16[1,1024,2,1024]{3,2,1,0:T(2,128)(2,1)}, u32[]{:S(2)}) %copy-start) | copy-done | bytes 4194328
  3.9 0.7 copy-done.5
  4.6 5.7 %encode_first.1 = (bf16[192,1024]{1,0:T(8,128)(2,1)S(1)}, bf16[64,1024]{1,0:T(8,128)(2,1)S(1)}, bf16[2048,1024]{1,0:T(8,128)(2,1)S(1)}) custom-call(s32[2]{0:T(128)S(1)} %pad_add_fusion.3.info_ref, s32[2,512]{1,0:T(2,128)S(1)} %copy-done.5, f32[2,2048]{1,0:T(2,128)S(1)} %mul.10.shot_ref, bf16[1024,2,1024]{2,1,0:T(2,128)(2,1)S(1)} %bitcast.20), custom_call_target="tpu_custom_call" | custom-call | flops 1073741824 | bytes 8388608 | tf_op jit(solution)/shard_map/encode_first/pallas_call | solution.py:143
  10.3 0.0 copy-start.1
  10.3 2.0 %copy-done.1 = bf16[2048,1024]{1,0:T(8,128)(2,1)} copy-done((bf16[2048,1024]{1,0:T(8,128)(2,1)}, bf16[2048,1024]{1,0:T(8,128)(2,1)S(1)}, u32[]{:S(2)}) %copy-start.1) | copy-done | bytes 4194328
  12.3 7.7 %collective-permute-start.6 = (bf16[64,1024]{1,0:T(8,128)(2,1)S(1)}, bf16[64,1024]{1,0:T(8,128)(2,1)S(1)}, u32[]{:S(2)}, u32[]{:S(2)}) collective-permute-start(bf16[64,1024]{1,0:T(8,128)(2,1)S(1)} %get-tuple-element.32), channel_id=1, source_target_pairs={{0,128},{1,129},{2,130},{3,131},{4,132},{5,133},{6,134},{7,135},{8... | collective-permute-start | bytes 393224 | tf_op jit(solution)/shard_map/ppermute | solution.py:67
  20.0 2.7 %collective-permute-start = (bf16[192,1024]{1,0:T(8,128)(2,1)S(1)}, bf16[192,1024]{1,0:T(8,128)(2,1)S(1)}, u32[]{:S(2)}, u32[]{:S(2)}) collective-permute-start(bf16[192,1024]{1,0:T(8,128)(2,1)S(1)} %get-tuple-element.24), channel_id=1, source_target_pairs={{0,32},{1,33},{2,34},{3,35},{4,36},{5,37},{6,38},{7,39},{8,40},{9,... | collective-permute-start | bytes 1179656 | tf_op jit(solution)/shard_map/ppermute | solution.py:67
  22.8 0.1 pad_add_fusion.4.info_ref
  22.8 0.0 copy-done.6
  22.9 2.2 %copy-done.2 = bf16[2048,1024]{1,0:T(8,128)(2,1)S(1)} copy-done((bf16[2048,1024]{1,0:T(8,128)(2,1)S(1)}, bf16[2048,1024]{1,0:T(8,128)(2,1)}, u32[]{:S(2)}) %copy-start.2) | copy-done | bytes 4194328
  25.0 9.0 %encode_later.3 = (bf16[192,1024]{1,0:T(8,128)(2,1)S(1)}, bf16[192,1024]{1,0:T(8,128)(2,1)S(1)}, bf16[64,1024]{1,0:T(8,128)(2,1)S(1)}, bf16[64,1024]{1,0:T(8,128)(2,1)S(1)}) custom-call(s32[4]{0:T(128)S(1)} %pad_add_fusion.4.info_ref, s32[2,512]{1,0:T(2,128)S(1)} %copy-done.6, f32[2,2048]{1,0:T(2,128)S(1)} %mul.10.shot_ref, bf16[2048,1024]{1,0:T(8,128)(2,1)S(1)} %copy-done.2), custom_call_target="tpu_custom_call" | custom-call | flops 2147483648 | bytes 8388608 | tf_op jit(solution)/shard_map/encode_later/pallas_call | solution.py:143
  34.1 0.1 collective-permute-start.7
  34.2 0.9 %collective-permute-start.1 = (bf16[192,1024]{1,0:T(8,128)(2,1)S(1)}, bf16[192,1024]{1,0:T(8,128)(2,1)S(1)}, u32[]{:S(2)}, u32[]{:S(2)}) collective-permute-start(bf16[192,1024]{1,0:T(8,128)(2,1)S(1)} %get-tuple-element.25), channel_id=1, source_target_pairs={{0,16},{1,49},{2,18},{3,51},{4,20},{5,53},{6,22},{7,55},{8,24},{9,... | collective-permute-start | bytes 1179656 | tf_op jit(solution)/shard_map/ppermute | solution.py:67
  35.1 0.6 collective-permute-start.2
  35.7 0.1 pad_add_fusion.2.info_ref
  35.8 0.0 collective-permute-done.6.refs_1_
  35.8 2.3 %collective-permute-start.8 = (bf16[64,1024]{1,0:T(8,128)(2,1)S(1)}, bf16[64,1024]{1,0:T(8,128)(2,1)S(1)}, u32[]{:S(2)}, u32[]{:S(2)}) collective-permute-start(bf16[64,1024]{1,0:T(8,128)(2,1)S(1)} %get-tuple-element.34), channel_id=1, source_target_pairs={{0,192},{1,65},{2,194},{3,67},{4,196},{5,69},{6,198},{7,71},{8,200... | collective-permute-start | bytes 393224 | tf_op jit(solution)/shard_map/ppermute | solution.py:67
  38.1 4.9 %encode_later.2 = (f32[192,1024]{1,0:T(8,128)S(1)}, f32[64,1024]{1,0:T(8,128)S(1)}) custom-call(s32[2]{0:T(128)S(1)} %pad_add_fusion.2.info_ref, s32[2,512]{1,0:T(2,128)S(1)} %copy-done.6, f32[2,2048]{1,0:T(2,128)S(1)} %mul.10.shot_ref, bf16[2048,1024]{1,0:T(8,128)(2,1)S(1)} %copy-done.2), custom_call_target="tpu_custom_call" | custom-call | flops 1073741824 | bytes 8388608 | tf_op jit(solution)/shard_map/encode_later/pallas_call | solution.py:143
  43.0 0.0 copy-start.3
  43.0 0.9 %copy-done.3 = f32[192,1024]{1,0:T(8,128)} copy-done((f32[192,1024]{1,0:T(8,128)}, f32[192,1024]{1,0:T(8,128)S(1)}, u32[]{:S(2)}) %copy-start.3) | copy-done | bytes 786456
  43.9 0.7 copy-done.4
  44.6 0.7 pad_add_fusion.5.info_ref
  45.2 0.0 collective-permute-done.7.refs_2_
  45.3 0.4 collective-permute-done.8.refs_3_
  45.6 0.0 copy-done.10
  45.6 0.3 copy-done.11
  45.9 0.4 copy-done.12
  46.3 1.8 %merge.3 = (bf16[16,1024]{1,0:T(8,128)(2,1)}, bf16[16,1024]{1,0:T(8,128)(2,1)}, bf16[16,1024]{1,0:T(8,128)(2,1)}, f32[16,1024]{1,0:T(8,128)}) custom-call(s32[4]{0:T(128)} %pad_add_fusion.5.info_ref, f32[64,1024]{1,0:T(8,128)} %copy-done.4, bf16[64,1024]{1,0:T(8,128)(2,1)} %copy-done.10, bf16[64,1024]{1,0:T(8,128)(2,1)} %copy-done.11, ...), custom_call_target="tpu_custom_call" | custom-call | tf_op jit(solution)/shard_map/merge/pallas_call | solution.py:168
  48.1 0.3 collective-permute-start.9
  48.4 0.7 pad_add_fusion.1.info_ref
  49.1 2.4 %collective-permute-start.10 = (bf16[16,1024]{1,0:T(8,128)(2,1)}, bf16[16,1024]{1,0:T(8,128)(2,1)S(1)}, u32[]{:S(2)}, u32[]{:S(2)}) collective-permute-start(bf16[16,1024]{1,0:T(8,128)(2,1)} %get-tuple-element.37), channel_id=1, source_target_pairs={{0,16},{1,49},{2,18},{3,51},{4,20},{5,53},{6,22},{7,55},{8,24},{9,... | collective-permute-start | bytes 98312 | tf_op jit(solution)/shard_map/ppermute | solution.py:67
  51.5 0.0 collective-permute-done.refs_1_
  51.5 0.0 collective-permute-start.11
  51.5 0.0 collective-permute-done.1.refs_2_
  51.5 0.0 copy-start.8
  51.5 0.0 collective-permute-done.2.refs_3_
  51.5 0.0 copy-start.9
  51.5 0.7 copy-done.7
  52.2 0.1 copy-done.8
  52.4 0.1 copy-done.9
  52.5 2.3 %merge.2 = (bf16[48,1024]{1,0:T(8,128)(2,1)}, bf16[48,1024]{1,0:T(8,128)(2,1)}, bf16[48,1024]{1,0:T(8,128)(2,1)}, f32[48,1024]{1,0:T(8,128)}) custom-call(s32[4]{0:T(128)} %pad_add_fusion.1.info_ref, f32[192,1024]{1,0:T(8,128)} %copy-done.3, bf16[192,1024]{1,0:T(8,128)(2,1)} %copy-done.7, bf16[192,1024]{1,0:T(8,128)(2,1)} %copy-done.8, ...), custom_call_target="tpu_custom_call" | custom-call | tf_op jit(solution)/shard_map/merge/pallas_call | solution.py:168
  54.8 2.0 %collective-permute-start.3 = (bf16[48,1024]{1,0:T(8,128)(2,1)}, bf16[48,1024]{1,0:T(8,128)(2,1)S(1)}, u32[]{:S(2)}, u32[]{:S(2)}) collective-permute-start(bf16[48,1024]{1,0:T(8,128)(2,1)} %get-tuple-element.28), channel_id=1, source_target_pairs={{0,128},{1,129},{2,130},{3,131},{4,132},{5,133},{6,134},{7,135},{8... | collective-permute-start | bytes 294920 | tf_op jit(solution)/shard_map/ppermute | solution.py:67
  56.9 3.3 %collective-permute-start.4 = (bf16[48,1024]{1,0:T(8,128)(2,1)}, bf16[48,1024]{1,0:T(8,128)(2,1)S(1)}, u32[]{:S(2)}, u32[]{:S(2)}) collective-permute-start(bf16[48,1024]{1,0:T(8,128)(2,1)} %get-tuple-element.29), channel_id=1, source_target_pairs={{0,64},{1,193},{2,66},{3,195},{4,68},{5,197},{6,70},{7,199},{8,72}... | collective-permute-start | bytes 294920 | tf_op jit(solution)/shard_map/ppermute | solution.py:67
  60.2 0.0 collective-permute-done.9.refs_5_
  60.2 0.0 collective-permute-start.5
  60.2 0.7 pad_add_fusion.info_ref
  60.9 0.0 collective-permute-done.10.refs_6_
  60.9 0.0 collective-permute-done.11.refs_7_
  60.9 0.0 copy-start.18
  60.9 2.6 %collective-permute-done.3.refs_1_ = bf16[48,1024]{1,0:T(8,128)(2,1)S(1)} collective-permute-done((bf16[48,1024]{1,0:T(8,128)(2,1)}, bf16[48,1024]{1,0:T(8,128)(2,1)S(1)}, u32[]{:S(2)}, u32[]{:S(2)}) %collective-permute-start.3) | collective-permute-done | bytes 98336 | tf_op jit(solution)/shard_map/ppermute | solution.py:67
  63.5 0.5 collective-permute-done.4.refs_2_
  64.0 5.7 %collective-permute-done.5.refs_3_ = bf16[48,1024]{1,0:T(8,128)(2,1)S(1)} collective-permute-done((bf16[48,1024]{1,0:T(8,128)(2,1)}, bf16[48,1024]{1,0:T(8,128)(2,1)S(1)}, u32[]{:S(2)}, u32[]{:S(2)}) %collective-permute-start.5) | collective-permute-done | bytes 98336 | tf_op jit(solution)/shard_map/ppermute | solution.py:67
  69.8 0.0 copy-done.16
  69.8 0.0 copy-done.17
  69.8 0.0 copy-done.18
  69.8 0.6 copy-done.15
  70.4 2.2 %last.1 = bf16[2,32,1024]{2,1,0:T(8,128)(2,1)} custom-call(s32[2]{0:T(128)} %pad_add_fusion.info_ref, s32[2,512]{1,0:T(2,128)} %ray_ref.7, s32[2,1024]{1,0:T(2,128)} %rcv_ref.1, f32[48,1024]{1,0:T(8,128)} %get-tuple-element.27.refs_0_, bf16[48,1024]{1,0:T(8,128)(2,1)} %copy-done.13, bf16[48,1024]{1,0:T(8,128)(2,1)} %copy-done.14, ...), custom_call_target="tpu_custom_call" | custom-call | tf_op jit(solution)/shard_map/last/pallas_call | solution.py:228
  72.6 1.0 %copy.7 = bf16[32,1,2,1024]{3,2,1,0:T(2,128)(2,1)S(1)} copy(bf16[32,1,2,1024]{3,0,2,1:T(8,128)(2,1)} %bitcast.22) | data formatting | bytes 262144 | tf_op jit(solution)/shard_map/reshape | solution.py:235
  73.6 13.1 %all_to_all.18 = bf16[32,1,2,1024]{3,2,1,0:T(2,128)(2,1)S(1)} all-to-all(bf16[32,1,2,1024]{3,2,1,0:T(2,128)(2,1)S(1)} %copy.7), channel_id=1, replica_groups=mesh['shot'=16,'rcv'=16] {'rcv'}, dimensions={0} | all-to-all | bytes 262144 | tf_op jit(solution)/shard_map/all_to_all | solution.py:236
  86.7 0.7 copy.10
  (16 shorter events, 0.0 us)
Async XLA Ops:
  0.0 22.8 %copy-start.6 = (s32[2,512]{1,0:T(2,128)S(1)}, s32[2,512]{1,0:T(2,128)}, u32[]{:S(2)}) copy-start(s32[2,512]{1,0:T(2,128)} %ray_ref.7) | copy-start | bytes 12292
  1.7 2.2 %copy-start = (bf16[1,1024,2,1024]{3,2,1,0:T(2,128)(2,1)S(1)}, bf16[1,1024,2,1024]{3,2,1,0:T(2,128)(2,1)}, u32[]{:S(2)}) copy-start(bf16[1,1024,2,1024]{3,2,1,0:T(2,128)(2,1)} %param.4) | copy-start | bytes 12582916
  3.9 0.7 copy-start.5
  10.3 2.0 %copy-start.1 = (bf16[2048,1024]{1,0:T(8,128)(2,1)}, bf16[2048,1024]{1,0:T(8,128)(2,1)S(1)}, u32[]{:S(2)}) copy-start(bf16[2048,1024]{1,0:T(8,128)(2,1)S(1)} %get-tuple-element.22.data_ref) | copy-start | bytes 12582916
  12.3 23.5 %collective-permute-start.6 = (bf16[64,1024]{1,0:T(8,128)(2,1)S(1)}, bf16[64,1024]{1,0:T(8,128)(2,1)S(1)}, u32[]{:S(2)}, u32[]{:S(2)}) collective-permute-start(bf16[64,1024]{1,0:T(8,128)(2,1)S(1)} %get-tuple-element.32), channel_id=1, source_target_pairs={{0,128},{1,129},{2,130},{3,131},{4,132},{5,133},{6,134},{7,135},{8... | collective-permute-start | bytes 393224 | tf_op jit(solution)/shard_map/ppermute | solution.py:67
  20.0 31.4 %collective-permute-start = (bf16[192,1024]{1,0:T(8,128)(2,1)S(1)}, bf16[192,1024]{1,0:T(8,128)(2,1)S(1)}, u32[]{:S(2)}, u32[]{:S(2)}) collective-permute-start(bf16[192,1024]{1,0:T(8,128)(2,1)S(1)} %get-tuple-element.24), channel_id=1, source_target_pairs={{0,32},{1,33},{2,34},{3,35},{4,36},{5,37},{6,38},{7,39},{8,40},{9,... | collective-permute-start | bytes 1179656 | tf_op jit(solution)/shard_map/ppermute | solution.py:67
  22.8 2.2 %copy-start.2 = (bf16[2048,1024]{1,0:T(8,128)(2,1)S(1)}, bf16[2048,1024]{1,0:T(8,128)(2,1)}, u32[]{:S(2)}) copy-start(bf16[2048,1024]{1,0:T(8,128)(2,1)} %copy-done.1) | copy-start | bytes 12582916
  34.1 11.2 %collective-permute-start.7 = (bf16[64,1024]{1,0:T(8,128)(2,1)S(1)}, bf16[64,1024]{1,0:T(8,128)(2,1)S(1)}, u32[]{:S(2)}, u32[]{:S(2)}) collective-permute-start(bf16[64,1024]{1,0:T(8,128)(2,1)S(1)} %get-tuple-element.33), channel_id=1, source_target_pairs={{0,64},{1,193},{2,66},{3,195},{4,68},{5,197},{6,70},{7,199},{8,72}... | collective-permute-start | bytes 393224 | tf_op jit(solution)/shard_map/ppermute | solution.py:67
  34.2 17.3 %collective-permute-start.1 = (bf16[192,1024]{1,0:T(8,128)(2,1)S(1)}, bf16[192,1024]{1,0:T(8,128)(2,1)S(1)}, u32[]{:S(2)}, u32[]{:S(2)}) collective-permute-start(bf16[192,1024]{1,0:T(8,128)(2,1)S(1)} %get-tuple-element.25), channel_id=1, source_target_pairs={{0,16},{1,49},{2,18},{3,51},{4,20},{5,53},{6,22},{7,55},{8,24},{9,... | collective-permute-start | bytes 1179656 | tf_op jit(solution)/shard_map/ppermute | solution.py:67
  35.1 16.4 %collective-permute-start.2 = (bf16[192,1024]{1,0:T(8,128)(2,1)S(1)}, bf16[192,1024]{1,0:T(8,128)(2,1)S(1)}, u32[]{:S(2)}, u32[]{:S(2)}) collective-permute-start(bf16[192,1024]{1,0:T(8,128)(2,1)S(1)} %get-tuple-element.26), channel_id=1, source_target_pairs={{0,48},{1,17},{2,50},{3,19},{4,52},{5,21},{6,54},{7,23},{8,56},{9,... | collective-permute-start | bytes 1179656 | tf_op jit(solution)/shard_map/ppermute | solution.py:67
  35.8 9.8 %copy-start.10 = (bf16[64,1024]{1,0:T(8,128)(2,1)}, bf16[64,1024]{1,0:T(8,128)(2,1)S(1)}, u32[]{:S(2)}) copy-start(bf16[64,1024]{1,0:T(8,128)(2,1)S(1)} %collective-permute-done.6.refs_1_) | copy-start | bytes 393220
  35.8 9.8 %collective-permute-start.8 = (bf16[64,1024]{1,0:T(8,128)(2,1)S(1)}, bf16[64,1024]{1,0:T(8,128)(2,1)S(1)}, u32[]{:S(2)}, u32[]{:S(2)}) collective-permute-start(bf16[64,1024]{1,0:T(8,128)(2,1)S(1)} %get-tuple-element.34), channel_id=1, source_target_pairs={{0,192},{1,65},{2,194},{3,67},{4,196},{5,69},{6,198},{7,71},{8,200... | collective-permute-start | bytes 393224 | tf_op jit(solution)/shard_map/ppermute | solution.py:67
  43.0 0.9 %copy-start.3 = (f32[192,1024]{1,0:T(8,128)}, f32[192,1024]{1,0:T(8,128)S(1)}, u32[]{:S(2)}) copy-start(f32[192,1024]{1,0:T(8,128)S(1)} %get-tuple-element.23.refs_0_) | copy-start | bytes 2359300
  43.9 0.7 copy-start.4
  45.2 0.6 copy-start.11
  45.6 0.7 copy-start.12
  48.1 12.1 %collective-permute-start.9 = (bf16[16,1024]{1,0:T(8,128)(2,1)}, bf16[16,1024]{1,0:T(8,128)(2,1)S(1)}, u32[]{:S(2)}, u32[]{:S(2)}) collective-permute-start(bf16[16,1024]{1,0:T(8,128)(2,1)} %get-tuple-element.36), channel_id=1, source_target_pairs={{0,32},{1,33},{2,34},{3,35},{4,36},{5,37},{6,38},{7,39},{8,40},{9,... | collective-permute-start | bytes 98312 | tf_op jit(solution)/shard_map/ppermute | solution.py:67
  49.1 11.8 %collective-permute-start.10 = (bf16[16,1024]{1,0:T(8,128)(2,1)}, bf16[16,1024]{1,0:T(8,128)(2,1)S(1)}, u32[]{:S(2)}, u32[]{:S(2)}) collective-permute-start(bf16[16,1024]{1,0:T(8,128)(2,1)} %get-tuple-element.37), channel_id=1, source_target_pairs={{0,16},{1,49},{2,18},{3,51},{4,20},{5,53},{6,22},{7,55},{8,24},{9,... | collective-permute-start | bytes 98312 | tf_op jit(solution)/shard_map/ppermute | solution.py:67
  51.5 0.8 copy-start.7
  51.5 9.4 %collective-permute-start.11 = (bf16[16,1024]{1,0:T(8,128)(2,1)}, bf16[16,1024]{1,0:T(8,128)(2,1)S(1)}, u32[]{:S(2)}, u32[]{:S(2)}) collective-permute-start(bf16[16,1024]{1,0:T(8,128)(2,1)} %get-tuple-element.38), channel_id=1, source_target_pairs={{0,48},{1,17},{2,50},{3,19},{4,52},{5,21},{6,54},{7,23},{8,56},{9,... | collective-permute-start | bytes 98312 | tf_op jit(solution)/shard_map/ppermute | solution.py:67
  51.5 0.9 %copy-start.8 = (bf16[192,1024]{1,0:T(8,128)(2,1)}, bf16[192,1024]{1,0:T(8,128)(2,1)S(1)}, u32[]{:S(2)}) copy-start(bf16[192,1024]{1,0:T(8,128)(2,1)S(1)} %collective-permute-done.1.refs_2_) | copy-start | bytes 1179652
  51.5 1.0 %copy-start.9 = (bf16[192,1024]{1,0:T(8,128)(2,1)}, bf16[192,1024]{1,0:T(8,128)(2,1)S(1)}, u32[]{:S(2)}) copy-start(bf16[192,1024]{1,0:T(8,128)(2,1)S(1)} %collective-permute-done.2.refs_3_) | copy-start | bytes 1179652
  54.8 8.6 %collective-permute-start.3 = (bf16[48,1024]{1,0:T(8,128)(2,1)}, bf16[48,1024]{1,0:T(8,128)(2,1)S(1)}, u32[]{:S(2)}, u32[]{:S(2)}) collective-permute-start(bf16[48,1024]{1,0:T(8,128)(2,1)} %get-tuple-element.28), channel_id=1, source_target_pairs={{0,128},{1,129},{2,130},{3,131},{4,132},{5,133},{6,134},{7,135},{8... | collective-permute-start | bytes 294920 | tf_op jit(solution)/shard_map/ppermute | solution.py:67
  56.9 7.1 %collective-permute-start.4 = (bf16[48,1024]{1,0:T(8,128)(2,1)}, bf16[48,1024]{1,0:T(8,128)(2,1)S(1)}, u32[]{:S(2)}, u32[]{:S(2)}) collective-permute-start(bf16[48,1024]{1,0:T(8,128)(2,1)} %get-tuple-element.29), channel_id=1, source_target_pairs={{0,64},{1,193},{2,66},{3,195},{4,68},{5,197},{6,70},{7,199},{8,72}... | collective-permute-start | bytes 294920 | tf_op jit(solution)/shard_map/ppermute | solution.py:67
  60.2 9.6 %copy-start.16 = (bf16[16,1024]{1,0:T(8,128)(2,1)}, bf16[16,1024]{1,0:T(8,128)(2,1)S(1)}, u32[]{:S(2)}) copy-start(bf16[16,1024]{1,0:T(8,128)(2,1)S(1)} %collective-permute-done.9.refs_5_) | copy-start | bytes 98308
  60.2 9.6 %collective-permute-start.5 = (bf16[48,1024]{1,0:T(8,128)(2,1)}, bf16[48,1024]{1,0:T(8,128)(2,1)S(1)}, u32[]{:S(2)}, u32[]{:S(2)}) collective-permute-start(bf16[48,1024]{1,0:T(8,128)(2,1)} %get-tuple-element.30), channel_id=1, source_target_pairs={{0,192},{1,65},{2,194},{3,67},{4,196},{5,69},{6,198},{7,71},{8,200... | collective-permute-start | bytes 294920 | tf_op jit(solution)/shard_map/ppermute | solution.py:67
  60.9 8.9 %copy-start.17 = (bf16[16,1024]{1,0:T(8,128)(2,1)}, bf16[16,1024]{1,0:T(8,128)(2,1)S(1)}, u32[]{:S(2)}) copy-start(bf16[16,1024]{1,0:T(8,128)(2,1)S(1)} %collective-permute-done.10.refs_6_) | copy-start | bytes 98308
  60.9 8.9 %copy-start.18 = (bf16[16,1024]{1,0:T(8,128)(2,1)}, bf16[16,1024]{1,0:T(8,128)(2,1)S(1)}, u32[]{:S(2)}) copy-start(bf16[16,1024]{1,0:T(8,128)(2,1)S(1)} %collective-permute-done.11.refs_7_) | copy-start | bytes 98308
  63.5 6.3 %copy-start.13 = (bf16[48,1024]{1,0:T(8,128)(2,1)}, bf16[48,1024]{1,0:T(8,128)(2,1)S(1)}, u32[]{:S(2)}) copy-start(bf16[48,1024]{1,0:T(8,128)(2,1)S(1)} %collective-permute-done.3.refs_1_) | copy-start | bytes 294916
  64.0 5.8 %copy-start.14 = (bf16[48,1024]{1,0:T(8,128)(2,1)}, bf16[48,1024]{1,0:T(8,128)(2,1)S(1)}, u32[]{:S(2)}) copy-start(bf16[48,1024]{1,0:T(8,128)(2,1)S(1)} %collective-permute-done.4.refs_2_) | copy-start | bytes 294916
  69.8 0.6 copy-start.15

commit v2 on v0

v2 whole, which is shorter than its diff:
```python
import functools
import math

import jax
import jax.numpy as jnp
import numpy as np
from jax import lax
from jax.experimental import pallas as pl
from jax.experimental.pallas import tpu as pltpu
from jax.sharding import PartitionSpec as P

BASE = 5
MODULUS = 1024
ZH, XS, ZL, YS, CORES = 4, 4, 2, 4, 2
SHOT, RCV = ZH * XS, ZL * YS * CORES
RAYS, WIDTH, LOCAL = 512, 1024, 1024
SHARE = RAYS // SHOT
XFIRST = 24
ZFIRST = SHARE - XFIRST
VMEM = pl.BlockSpec(memory_space=pltpu.VMEM)
SMEM = pl.BlockSpec(memory_space=pltpu.SMEM)
STEPS = ((2, 2), (1, 3), (3, 1), (0, 0))
F32, BF16 = jnp.float32, jnp.bfloat16


def fitted(fn, degree):
    points = 0.125 * (1 + np.cos(np.pi * (np.arange(400) + 0.5) / 400))
    series = np.polynomial.chebyshev.Chebyshev.fit(points, fn(np.sqrt(points)), degree, domain=[0, 0.25])
    return [float(a) for a in series.convert(kind=np.polynomial.Polynomial).coef]


HALF_COS = fitted(lambda f: np.cos(np.pi * f), 4)
HALF_SIN = fitted(lambda f: np.sin(np.pi * f) / f, 3)


def horner(coefs, v):
    total = v * coefs[-1] + coefs[-2]
    for a in coefs[-3::-1]:
        total = total * v + a
    return total


def cos_minus_sin(turns):
    f = turns - jnp.round(turns)
    v = f * f
    s = f * horner(HALF_SIN, v)
    twice = s * -2.0
    return twice * s + 1.0, twice * horner(HALF_COS, v)


def iota(shape, axis):
    return lax.broadcasted_iota(jnp.int32, shape, axis)


def position(ref):
    return ref[0], ref[1], ref[2], ref[3]


def goal(at, core, step):
    return (at + jnp.where(core == 0, step[0], step[1])) % 4


def ray_columns(ray_ref):
    row = iota((8, RAYS), 0)
    r0, r1 = ray_ref[0:1, :].astype(F32), ray_ref[1:2, :].astype(F32)
    return jnp.where(row < 2, r0, jnp.where(row < 4, r1, jnp.where(row == 4, 1.0, 0.0))).astype(BF16)


def picked(columns, row_of_lane, rows, wave):
    chosen = (iota((rows, RAYS), 0) == row_of_lane).astype(BF16)
    p = lax.dot_general(chosen, columns, (((1,), (1,)), ((), ())), preferred_element_type=F32)
    col = iota((rows, 8), 1)
    p = jnp.where(col < 4, p * (wave.astype(F32) / MODULUS), p)
    high = p.astype(BF16).astype(F32)
    return jnp.where((col == 1) | (col == 3), p - high, high).astype(BF16)


def grid_rows(grid_ref, shots_ref):
    row = iota((8, LOCAL), 0)
    g = jnp.where(row < 2, grid_ref[0:1, :], jnp.where(row < 4, grid_ref[1:2, :], 0)).astype(F32).astype(BF16)
    twice = (iota((128, 256), 0) == iota((128, 256), 1) // 2).astype(BF16)
    quarter = jnp.where(iota((8, 256), 0) == 4, (iota((8, 256), 1) % 2).astype(F32) * -0.25, 0.0)
    for i in range(LOCAL // 128):
        wide = jnp.dot(g[:, i * 128 : (i + 1) * 128], twice, preferred_element_type=F32) + quarter
        shots_ref[:, i * 256 : (i + 1) * 256] = wide.astype(BF16)


def phase_rows(group, where, columns, shots_ref, lhs, base, chunk=256):
    axis, low, m, step = group
    zh, x, core, wave = where
    lane = iota((1, RAYS), 1)
    zh_of, x_of, q_of = lane // (RAYS // ZH), lane // SHARE % XS, lane % SHARE
    along, other, at = (x_of, zh_of, x) if axis == "x" else (zh_of, x_of, zh)
    mine = (along == goal(at, core, step)) & (q_of >= low) & (q_of < low + m)
    p = picked(columns, jnp.where(mine, other * m + q_of - low, -1), 4 * m, wave)
    for k in range(0, 2 * LOCAL, chunk):
        c, s = cos_minus_sin(jnp.dot(p, shots_ref[:, k : k + chunk], preferred_element_type=F32))
        for i in range(4):
            unit = jnp.concatenate([c[i * m : (i + 1) * m], s[i * m : (i + 1) * m]], 0)
            lhs[base + 2 * m * i : base + 2 * m * (i + 1), k : k + chunk] = unit.astype(BF16)


def products(rows, lhs, base, data_ref, out):
    for i in range(0, WIDTH, 256):
        r = jnp.dot(lhs[base : base + rows], data_ref[:, i : i + 256], preferred_element_type=F32)
        out[:, i : i + 256] = r.astype(out.dtype)


def first_kernel(groups, place_ref, ray_ref, grid_ref, x_ref, *refs):
    outs, (data_ref, shots_ref, lhs, buf, ray_buf, grid_buf, sems) = refs[: len(groups)], refs[len(groups) :]
    small = [pltpu.make_async_copy(ray_ref, ray_buf, sems.at[8]), pltpu.make_async_copy(grid_ref, grid_buf, sems.at[9])]
    for copy in small:
        copy.start()
    part = LOCAL // 8
    copies = []
    for i in range(8):
        at = pl.ds(i * part, part)
        copies.append(pltpu.make_async_copy(x_ref.at[at], buf.at[at], sems.at[i]))
        copies[-1].start()
    for copy in small:
        copy.wait()
    where = position(place_ref)
    columns = ray_columns(ray_buf)
    grid_rows(grid_buf, shots_ref)
    base = 0
    for group in groups:
        phase_rows(group, where, columns, shots_ref, lhs, base)
        base += 8 * group[2]
    for i in range(8):
        copies[i].wait()
        for s in range(i * part, (i + 1) * part, 8):
            data_ref[2 * s : 2 * s + 16] = buf[s : s + 8].reshape(16, WIDTH)
    base = 0
    for group, out in zip(groups, outs):
        products(8 * group[2], lhs, base, data_ref, out)
        base += 8 * group[2]


def later_kernel(groups, place_ref, ray_ref, shots_ref, data_ref, *refs):
    outs, (lhs,) = refs[: len(groups)], refs[len(groups) :]
    where = position(place_ref)
    columns = ray_columns(ray_ref)
    base = 0
    for group, out in zip(groups, outs):
        phase_rows(group, where, columns, shots_ref, lhs, base)
        products(8 * group[2], lhs, base, data_ref, out)
        base += 8 * group[2]


def encode(groups, spot, ray_table, shots, x, dtype, first):
    rows = sum(8 * g[2] for g in groups)
    shapes = [jax.ShapeDtypeStruct((8 * g[2], WIDTH), dtype) for g in groups]
    scratch = [pltpu.VMEM((rows, 2 * LOCAL), BF16)]
    if first:
        shapes += [jax.ShapeDtypeStruct((2 * LOCAL, WIDTH), BF16), jax.ShapeDtypeStruct((8, 2 * LOCAL), BF16)]
        scratch += [pltpu.VMEM((LOCAL, 2, WIDTH), BF16), pltpu.VMEM((2, RAYS), jnp.int32), pltpu.VMEM((2, LOCAL), jnp.int32)]
        scratch += [pltpu.SemaphoreType.DMA((10,))]
    if first:
        ray_table, shots, x = (pltpu.with_memory_space_constraint(a, pltpu.HBM) for a in (ray_table, shots, x))
    return pl.pallas_call(
        functools.partial(first_kernel if first else later_kernel, groups),
        out_shape=shapes,
        in_specs=[SMEM] + ([pl.BlockSpec(memory_space=pltpu.HBM)] * 3 if first else [VMEM] * 3),
        out_specs=[VMEM] * len(shapes),
        scratch_shapes=scratch,
        compiler_params=pltpu.CompilerParams(vmem_limit_bytes=20 * 2**20),
        cost_estimate=pl.CostEstimate(flops=2 * rows * 2 * LOCAL * WIDTH, bytes_accessed=8 * 2**20, transcendentals=0),
        name="encode_first" if first else "encode_later",
    )(spot, ray_table, shots, x)


def place(index):
    shot, rcv = index // RCV, index % RCV
    return shot // XS, shot % XS, rcv // (YS * CORES), rcv // CORES % YS, rcv % CORES


def joined(zh, x, zl, y, core):
    return ((zh % ZH) * XS + x % XS) * RCV + (zl * YS + y) * CORES + core


def send(value, axis, steps):
    pairs = []
    for index in range(SHOT * RCV):
        zh, x, zl, y, core = place(index)
        step = steps[core]
        pairs.append((index, joined(zh + step, x, zl, y, core) if axis == "z" else joined(zh, x + step, zl, y, core)))
    return lax.ppermute(value, ("shot", "rcv"), pairs)


def merge_kernel(axis, place_ref, own, *refs):
    ins, outs = refs[:3], refs[3:]
    zh, x, core, _ = position(place_ref)
    unit = own.shape[0] // 4
    for step, out in zip(STEPS, outs):
        at = pl.ds(pl.multiple_of(goal(zh if axis == "x" else x, core, step) * unit, 16), unit)
        total = own[at, :]
        for piece in ins:
            total = total + piece[at, :].astype(F32)
        out[...] = total.astype(out.dtype)


def merge(axis, spot, own, received):
    unit = own.shape[0] // 4
    return pl.pallas_call(
        functools.partial(merge_kernel, axis),
        out_shape=[jax.ShapeDtypeStruct((unit, WIDTH), d) for d in (BF16, BF16, BF16, F32)],
        in_specs=[SMEM] + [VMEM] * 4,
        out_specs=[VMEM] * 4,
        compiler_params=pltpu.CompilerParams(vmem_limit_bytes=12 * 2**20),
        name="merge_" + axis,
    )(spot, own, *received)


def last_kernel(scale, place_ref, ray_ref, rcv_ref, *refs):
    ins, (out, rows) = refs[:8], refs[8:]
    zh, x, core, wave = position(place_ref)
    shot = zh * XS + x
    row = iota((8, WIDTH), 0)
    grid = jnp.where(row < 2, rcv_ref[0:1, :], jnp.where(row < 4, rcv_ref[1:2, :], 0)).astype(F32).astype(BF16)
    p = picked(ray_columns(ray_ref), iota((1, RAYS), 1) - shot * SHARE, SHARE, wave)
    for i in range(0, WIDTH, 256):
        at = slice(i, i + 256)
        c, s = cos_minus_sin(jnp.dot(p, grid[:, at], preferred_element_type=F32))
        parts = []
        for some in (ins[:4], ins[4:]):
            total = some[0][:, at]
            for piece in some[1:]:
                total = total + piece[:, at].astype(F32)
            parts.append(total)
        re = jnp.concatenate([parts[0][:XFIRST], parts[1][:ZFIRST]], 0)
        im = jnp.concatenate([parts[0][XFIRST:], parts[1][ZFIRST:]], 0)
        turned = (scale * (re * c + im * s), scale * (im * c - re * s))
        for k in range(2):
            for j in range(i, i + 256, 128):
                rows[j // 128, pl.ds(k, SHARE, stride=2), :] = turned[k][:, j - i : j - i + 128]
        for j in range(i, i + 256, 128):
            out[:, j : j + 128] = rows[j // 128].astype(BF16)


def last(scale, spot, ray_table, receiver_grid, ins):
    return pl.pallas_call(
        functools.partial(last_kernel, scale),
        out_shape=jax.ShapeDtypeStruct((2 * SHARE, WIDTH), BF16),
        in_specs=[SMEM] + [VMEM] * 10,
        out_specs=VMEM,
        scratch_shapes=[pltpu.VMEM((WIDTH // 128, 2 * SHARE, 128), F32)],
        compiler_params=pltpu.CompilerParams(vmem_limit_bytes=8 * 2**20),
        name="last",
    )(spot, ray_table, receiver_grid, *ins)


def on_device(spectra, shot_grid, ray_table, receiver_grid):
    scale = 1.0 / math.sqrt(LOCAL * SHOT)
    shot, rcv = lax.axis_index("shot"), lax.axis_index("rcv")
    spot = jnp.stack([shot // XS, shot % XS, rcv % CORES, BASE + rcv]).astype(jnp.int32)
    px, qz = ("x", 0, XFIRST), ("z", XFIRST, ZFIRST)
    groups = [[px + (s,) for s in STEPS], [qz + (s,) for s in STEPS]]
    p0, q0, data, shots = encode([g[0] for g in groups], spot, ray_table, shot_grid, spectra.reshape(LOCAL, 2, WIDTH), BF16, True)
    from_x, from_z = [send(p0, "x", STEPS[0])], [send(q0, "z", STEPS[0])]
    p1, p2, q1, q2 = encode(groups[0][1:3] + groups[1][1:3], spot, ray_table, shots, data, BF16, False)
    from_x += [send(p1, "x", STEPS[1]), send(p2, "x", STEPS[2])]
    from_z += [send(q1, "z", STEPS[1]), send(q2, "z", STEPS[2])]
    shots, p1 = lax.optimization_barrier((shots, p1))
    p3, q3 = encode([g[3] for g in groups], spot, ray_table, shots, data, F32, False)
    half = merge("x", spot, p3, from_x)
    other = merge("z", spot, q3, from_z)
    ins = [half[3]] + [send(half[k], "z", STEPS[k]) for k in range(3)]
    ins += [other[3]] + [send(other[k], "x", STEPS[k]) for k in range(3)]
    turned = last(scale, spot, ray_table, receiver_grid, ins)
    return lax.all_to_all(turned.reshape(SHARE, 1, 2, WIDTH), "rcv", split_axis=0, concat_axis=1, tiled=True)


def solution(mesh):
    in_specs = (P("rcv", "shot", None, None), P(None, "shot"), P(), P())
    out_specs = P(("shot", "rcv"), None, None, None)
    return jax.shard_map(on_device, mesh=mesh, in_specs=in_specs, out_specs=out_specs, check_vma=False)
```

time: 279 us -> 62.7 us (0.22)
  waiting for transfers between devices: 220 us -> 4.29 us
  starting transfers between devices: 0.01 us -> 26.9 us
  Pallas kernels: 0 us -> 15.9 us
  other arithmetic: 14.5 us -> 0.08 us
  between operations: 13.4 us -> 0.08 us
  local copies, waits for them, and re-layouts: 8.76 us -> 0.81 us
  matrix products: 6.29 us -> 0 us
    psum x1 -> x0, waiting for transfers between devices: 219 us -> none  [on_device(): summed = lax.psum(jnp.stack(pieces, 1), 'shot')]
    ppermute x0 -> x12, starting transfers between devices: none -> 26.9 us  [send(): return lax.ppermute(value, ('shot', 'rcv'), pairs)]
    pallas_call x0 -> x6, Pallas kernels: none -> 15.9 us  [the longest x3 13.6 us: encode(): pl.pallas_call(functools.partial(first_kernel if first else later_kernel,...]
    another operation x5 -> x1, other arithmetic: 14.5 us -> 0.08 us  [on_device(): jnp.stack([shot // XS, shot % XS, rcv % CORES, BASE + rcv])]
    dot_general x1 -> x0, matrix products: 6.29 us -> none  [on_device(): jnp.dot(phases, local_data[offset], preferred_element_type=jnp.float32)]
    unnamed x3 -> x4, local copies, waits for them, and re-layouts: 5.56 us -> 0.01 us
    ppermute x0 -> x12, waiting for transfers between devices: none -> 4.29 us  [send(): return lax.ppermute(value, ('shot', 'rcv'), pairs)]
  transfers between devices with their start and end apart: 1 -> 12, of which waited for: 1 -> 3; matrix products, arithmetic and copies ran while one was open for 0% -> 0% of each run, Pallas kernels for 0% -> 16%
where the time goes in v2:
time: 62.7 us; the launch traced here: 62.6 us
  starting transfers between devices  26.9 us (43%)
  Pallas kernels  15.9 us (25%)
  blocking collectives  14.6 us (23%)
  waiting for transfers between devices  4.29 us (7%)
  local copies, waits for them, and re-layouts  0.81 us (1%)
    ppermute x12, starting transfers between devices, send(): return lax.ppermute(value, ('shot', 'rcv'), pairs)  26.9 us
    all_to_all x1, blocking collectives, on_device(): lax.all_to_all(turned.reshape(SHARE, 1, 2, WIDTH), 'rcv', split_axis=0, c...  14.6 us
    pallas_call x3, Pallas kernels, encode(): pl.pallas_call(functools.partial(first_kernel if first else later_kernel,...  13.6 us
    ppermute x12, waiting for transfers between devices, send(): return lax.ppermute(value, ('shot', 'rcv'), pairs)  4.29 us
    pallas_call x2, Pallas kernels, merge(): pl.pallas_call(functools.partial(merge_kernel, axis), out_shape=[jax.Shap...  1.33 us
  transfers between devices with their start and end apart: 12, of which 3 were waited for; matrix products, arithmetic and copies ran while one was open for 0% of the time, Pallas kernels for 16%

profile of v2, /device:TPU:1, one launch (start us, length us, event | category | flops | bytes accessed | tf_op | source)
XLA Modules:
  0.0 62.6 jit_solution(10862214176769936720)
XLA Ops:
  0.0 0.0 copy-start
  0.0 0.1 pad_add_fusion.place_ref
  0.1 4.6 %encode_first.1 = (bf16[192,1024]{1,0:T(8,128)(2,1)S(1)}, bf16[64,1024]{1,0:T(8,128)(2,1)S(1)}, bf16[2048,1024]{1,0:T(8,128)(2,1)S(1)}, bf16[8,2048]{1,0:T(8,128)(2,1)S(1)}) custom-call(s32[4]{0:T(128)S(1)} %pad_add_fusion.place_ref, s32[2,512]{1,0:T(2,128)} %ray_ref.7, s32[2,1024]{1,0:T(2,128)} %grid_ref.1, bf16[1024,2,1024]{2,1,0:T(2,128)(2,1)} %bitcast.11), custom_call_target="tpu_custom_call" | custom-call | flops 1073741824 | bytes 8388608 | tf_op jit(solution)/shard_map/encode_first/pallas_call | solution.py:160
  4.7 3.7 %collective-permute-start = (bf16[192,1024]{1,0:T(8,128)(2,1)S(1)}, bf16[192,1024]{1,0:T(8,128)(2,1)S(1)}, u32[]{:S(2)}, u32[]{:S(2)}) collective-permute-start(bf16[192,1024]{1,0:T(8,128)(2,1)S(1)} %get-tuple-element.29), channel_id=1, source_target_pairs={{0,32},{1,33},{2,34},{3,35},{4,36},{5,37},{6,38},{7,39},{8,40},{9,... | collective-permute-start | bytes 1179656 | tf_op jit(solution)/shard_map/ppermute | solution.py:187
  8.4 0.0 copy-done
  8.4 5.7 %encode_later.2 = (bf16[192,1024]{1,0:T(8,128)(2,1)S(1)}, bf16[192,1024]{1,0:T(8,128)(2,1)S(1)}, bf16[64,1024]{1,0:T(8,128)(2,1)S(1)}, bf16[64,1024]{1,0:T(8,128)(2,1)S(1)}) custom-call(s32[4]{0:T(128)S(1)} %pad_add_fusion.place_ref, s32[2,512]{1,0:T(2,128)S(1)} %copy-done, bf16[8,2048]{1,0:T(8,128)(2,1)S(1)} %get-tuple-element.27.shots_ref, ...), custom_call_target="tpu_custom_call" | custom-call | flops 2147483648 | bytes 8388608 | tf_op jit(solution)/shard_map/encode_later/pallas_call | solution.py:160
  14.1 0.0 copy-start.1
  14.1 0.4 collective-permute-start.2
  14.5 2.4 %collective-permute-start.1 = (bf16[192,1024]{1,0:T(8,128)(2,1)S(1)}, bf16[192,1024]{1,0:T(8,128)(2,1)S(1)}, u32[]{:S(2)}, u32[]{:S(2)}) collective-permute-start(bf16[192,1024]{1,0:T(8,128)(2,1)S(1)} %get-tuple-element.26), channel_id=1, source_target_pairs={{0,16},{1,49},{2,18},{3,51},{4,20},{5,53},{6,22},{7,55},{8,24},{9,... | collective-permute-start | bytes 1179656 | tf_op jit(solution)/shard_map/ppermute | solution.py:187
  16.8 6.9 %collective-permute-start.6 = (bf16[64,1024]{1,0:T(8,128)(2,1)S(1)}, bf16[64,1024]{1,0:T(8,128)(2,1)S(1)}, u32[]{:S(2)}, u32[]{:S(2)}) collective-permute-start(bf16[64,1024]{1,0:T(8,128)(2,1)S(1)} %get-tuple-element.36), channel_id=1, source_target_pairs={{0,128},{1,129},{2,130},{3,131},{4,132},{5,133},{6,134},{7,135},{8... | collective-permute-start | bytes 393224 | tf_op jit(solution)/shard_map/ppermute | solution.py:187
  23.7 0.0 collective-permute-start.7
  23.7 0.0 collective-permute-done.refs_0_
  23.7 2.4 %collective-permute-start.8 = (bf16[64,1024]{1,0:T(8,128)(2,1)S(1)}, bf16[64,1024]{1,0:T(8,128)(2,1)S(1)}, u32[]{:S(2)}, u32[]{:S(2)}) collective-permute-start(bf16[64,1024]{1,0:T(8,128)(2,1)S(1)} %get-tuple-element.38), channel_id=1, source_target_pairs={{0,192},{1,65},{2,194},{3,67},{4,196},{5,69},{6,198},{7,71},{8,200... | collective-permute-start | bytes 393224 | tf_op jit(solution)/shard_map/ppermute | solution.py:187
  26.1 3.3 %encode_later.3 = (f32[192,1024]{1,0:T(8,128)S(1)}, f32[64,1024]{1,0:T(8,128)S(1)}) custom-call(s32[4]{0:T(128)S(1)} %pad_add_fusion.place_ref, s32[2,512]{1,0:T(2,128)S(1)} %copy-done, bf16[8,2048]{1,0:T(8,128)(2,1)S(1)} %get-tuple-element.27.shots_ref, bf16[2048,1024]{1,0:T(8,128)(2,1)S(1)} %get-tuple-element.25.data_ref), custom_call_target="tpu_custom_call" | custom-call | flops 1073741824 | bytes 8388608 | tf_op jit(solution)/shard_map/encode_later/pallas_call | solution.py:160
  29.4 0.0 collective-permute-done.2.refs_2_
  29.4 0.0 collective-permute-done.1.refs_1_
  29.4 0.7 %merge_x.1 = (bf16[48,1024]{1,0:T(8,128)(2,1)S(1)}, bf16[48,1024]{1,0:T(8,128)(2,1)S(1)}, bf16[48,1024]{1,0:T(8,128)(2,1)S(1)}, f32[48,1024]{1,0:T(8,128)S(1)}) custom-call(s32[4]{0:T(128)S(1)} %pad_add_fusion.place_ref, f32[192,1024]{1,0:T(8,128)S(1)} %get-tuple-element.28.own, bf16[192,1024]{1,0:T(8,128)(2,1)S(1)} %collective-permute-done.refs_0_, ...), custom_call_target="tpu_custom_call" | custom-call | tf_op jit(solution)/shard_map/merge_x/pallas_call | solution.py:204
  30.2 3.7 %collective-permute-start.3 = (bf16[48,1024]{1,0:T(8,128)(2,1)S(1)}, bf16[48,1024]{1,0:T(8,128)(2,1)S(1)}, u32[]{:S(2)}, u32[]{:S(2)}) collective-permute-start(bf16[48,1024]{1,0:T(8,128)(2,1)S(1)} %get-tuple-element.32), channel_id=1, source_target_pairs={{0,128},{1,129},{2,130},{3,131},{4,132},{5,133},{6,134},{7,135},{8... | collective-permute-start | bytes 294920 | tf_op jit(solution)/shard_map/ppermute | solution.py:187
  33.9 2.1 %collective-permute-start.4 = (bf16[48,1024]{1,0:T(8,128)(2,1)S(1)}, bf16[48,1024]{1,0:T(8,128)(2,1)S(1)}, u32[]{:S(2)}, u32[]{:S(2)}) collective-permute-start(bf16[48,1024]{1,0:T(8,128)(2,1)S(1)} %get-tuple-element.33), channel_id=1, source_target_pairs={{0,64},{1,193},{2,66},{3,195},{4,68},{5,197},{6,70},{7,199},{8,72}... | collective-permute-start | bytes 294920 | tf_op jit(solution)/shard_map/ppermute | solution.py:187
  35.9 0.0 collective-permute-done.6.refs_0_
  35.9 0.3 collective-permute-start.5
  36.2 0.4 collective-permute-done.7.refs_1_
  36.6 0.0 collective-permute-done.8.refs_2_
  36.6 0.6 merge_z.1
  37.2 2.6 %collective-permute-start.9 = (bf16[16,1024]{1,0:T(8,128)(2,1)S(1)}, bf16[16,1024]{1,0:T(8,128)(2,1)S(1)}, u32[]{:S(2)}, u32[]{:S(2)}) collective-permute-start(bf16[16,1024]{1,0:T(8,128)(2,1)S(1)} %get-tuple-element.40), channel_id=1, source_target_pairs={{0,32},{1,33},{2,34},{3,35},{4,36},{5,37},{6,38},{7,39},{8,40},{9,... | collective-permute-start | bytes 98312 | tf_op jit(solution)/shard_map/ppermute | solution.py:187
  39.8 1.2 %collective-permute-start.10 = (bf16[16,1024]{1,0:T(8,128)(2,1)S(1)}, bf16[16,1024]{1,0:T(8,128)(2,1)S(1)}, u32[]{:S(2)}, u32[]{:S(2)}) collective-permute-start(bf16[16,1024]{1,0:T(8,128)(2,1)S(1)} %get-tuple-element.41), channel_id=1, source_target_pairs={{0,16},{1,49},{2,18},{3,51},{4,20},{5,53},{6,22},{7,55},{8,24},{9,... | collective-permute-start | bytes 98312 | tf_op jit(solution)/shard_map/ppermute | solution.py:187
  41.0 0.9 %collective-permute-done.9.refs_5_ = bf16[16,1024]{1,0:T(8,128)(2,1)S(1)} collective-permute-done((bf16[16,1024]{1,0:T(8,128)(2,1)S(1)}, bf16[16,1024]{1,0:T(8,128)(2,1)S(1)}, u32[]{:S(2)}, u32[]{:S(2)}) %collective-permute-start.9) | collective-permute-done | bytes 32800 | tf_op jit(solution)/shard_map/ppermute | solution.py:187
  41.9 1.3 %collective-permute-start.11 = (bf16[16,1024]{1,0:T(8,128)(2,1)S(1)}, bf16[16,1024]{1,0:T(8,128)(2,1)S(1)}, u32[]{:S(2)}, u32[]{:S(2)}) collective-permute-start(bf16[16,1024]{1,0:T(8,128)(2,1)S(1)} %get-tuple-element.42), channel_id=1, source_target_pairs={{0,48},{1,17},{2,50},{3,19},{4,52},{5,21},{6,54},{7,23},{8,56},{9,... | collective-permute-start | bytes 98312 | tf_op jit(solution)/shard_map/ppermute | solution.py:187
  43.2 0.0 collective-permute-done.10.refs_6_
  43.2 3.0 %collective-permute-done.11.refs_7_ = bf16[16,1024]{1,0:T(8,128)(2,1)S(1)} collective-permute-done((bf16[16,1024]{1,0:T(8,128)(2,1)S(1)}, bf16[16,1024]{1,0:T(8,128)(2,1)S(1)}, u32[]{:S(2)}, u32[]{:S(2)}) %collective-permute-start.11) | collective-permute-done | bytes 32800 | tf_op jit(solution)/shard_map/ppermute | solution.py:187
  46.2 0.0 collective-permute-done.3.refs_1_
  46.2 0.0 collective-permute-done.4.refs_2_
  46.2 0.0 collective-permute-done.5.refs_3_
  46.2 0.0 copy-done.1
  46.2 1.0 %last.1 = bf16[64,1024]{1,0:T(8,128)(2,1)S(1)} custom-call(s32[4]{0:T(128)S(1)} %pad_add_fusion.place_ref, s32[2,512]{1,0:T(2,128)S(1)} %copy-done, s32[2,1024]{1,0:T(2,128)S(1)} %copy-done.1, f32[48,1024]{1,0:T(8,128)S(1)} %get-tuple-element.31.refs_0_, bf16[48,1024]{1,0:T(8,128)(2,1)S(1)} %collective-permute-done.3.refs_1_, ...), custom_call_target="tpu_custom_call" | custom-call | tf_op jit(solution)/shard_map/last/pallas_call | solution.py:241
  47.3 0.1 reshape.7
  47.3 14.6 %all_to_all.18 = bf16[32,1,2,1024]{3,2,1,0:T(2,128)(2,1)S(1)} all-to-all(bf16[32,1,2,1024]{3,2,1,0:T(2,128)(2,1)S(1)} %bitcast.12), channel_id=1, replica_groups=mesh['shot'=16,'rcv'=16] {'rcv'}, dimensions={0} | all-to-all | bytes 262144 | tf_op jit(solution)/shard_map/all_to_all | solution.py:270
  61.9 0.7 %copy.7 = bf16[2,16,2,1024]{3,2,1,0:T(2,128)(2,1)} copy(bf16[2,16,2,1024]{3,2,0,1:T(2,128)(2,1)S(1)} %bitcast.13) | data formatting | bytes 262144 | tf_op jit(solution)/shard_map/all_to_all | solution.py:270
Async XLA Ops:
  0.0 8.4 %copy-start = (s32[2,512]{1,0:T(2,128)S(1)}, s32[2,512]{1,0:T(2,128)}, u32[]{:S(2)}) copy-start(s32[2,512]{1,0:T(2,128)} %ray_ref.7) | copy-start | bytes 12292
  4.7 19.0 %collective-permute-start = (bf16[192,1024]{1,0:T(8,128)(2,1)S(1)}, bf16[192,1024]{1,0:T(8,128)(2,1)S(1)}, u32[]{:S(2)}, u32[]{:S(2)}) collective-permute-start(bf16[192,1024]{1,0:T(8,128)(2,1)S(1)} %get-tuple-element.29), channel_id=1, source_target_pairs={{0,32},{1,33},{2,34},{3,35},{4,36},{5,37},{6,38},{7,39},{8,40},{9,... | collective-permute-start | bytes 1179656 | tf_op jit(solution)/shard_map/ppermute | solution.py:187
  14.1 32.2 %copy-start.1 = (s32[2,1024]{1,0:T(2,128)S(1)}, s32[2,1024]{1,0:T(2,128)}, u32[]{:S(2)}) copy-start(s32[2,1024]{1,0:T(2,128)} %rcv_ref.1) | copy-start | bytes 24580
  14.1 15.3 %collective-permute-start.2 = (bf16[192,1024]{1,0:T(8,128)(2,1)S(1)}, bf16[192,1024]{1,0:T(8,128)(2,1)S(1)}, u32[]{:S(2)}, u32[]{:S(2)}) collective-permute-start(bf16[192,1024]{1,0:T(8,128)(2,1)S(1)} %get-tuple-element.30), channel_id=1, source_target_pairs={{0,48},{1,17},{2,50},{3,19},{4,52},{5,21},{6,54},{7,23},{8,56},{9,... | collective-permute-start | bytes 1179656 | tf_op jit(solution)/shard_map/ppermute | solution.py:187
  14.5 15.0 %collective-permute-start.1 = (bf16[192,1024]{1,0:T(8,128)(2,1)S(1)}, bf16[192,1024]{1,0:T(8,128)(2,1)S(1)}, u32[]{:S(2)}, u32[]{:S(2)}) collective-permute-start(bf16[192,1024]{1,0:T(8,128)(2,1)S(1)} %get-tuple-element.26), channel_id=1, source_target_pairs={{0,16},{1,49},{2,18},{3,51},{4,20},{5,53},{6,22},{7,55},{8,24},{9,... | collective-permute-start | bytes 1179656 | tf_op jit(solution)/shard_map/ppermute | solution.py:187
  16.8 19.1 %collective-permute-start.6 = (bf16[64,1024]{1,0:T(8,128)(2,1)S(1)}, bf16[64,1024]{1,0:T(8,128)(2,1)S(1)}, u32[]{:S(2)}, u32[]{:S(2)}) collective-permute-start(bf16[64,1024]{1,0:T(8,128)(2,1)S(1)} %get-tuple-element.36), channel_id=1, source_target_pairs={{0,128},{1,129},{2,130},{3,131},{4,132},{5,133},{6,134},{7,135},{8... | collective-permute-start | bytes 393224 | tf_op jit(solution)/shard_map/ppermute | solution.py:187
  23.7 12.9 %collective-permute-start.7 = (bf16[64,1024]{1,0:T(8,128)(2,1)S(1)}, bf16[64,1024]{1,0:T(8,128)(2,1)S(1)}, u32[]{:S(2)}, u32[]{:S(2)}) collective-permute-start(bf16[64,1024]{1,0:T(8,128)(2,1)S(1)} %get-tuple-element.37), channel_id=1, source_target_pairs={{0,64},{1,193},{2,66},{3,195},{4,68},{5,197},{6,70},{7,199},{8,72}... | collective-permute-start | bytes 393224 | tf_op jit(solution)/shard_map/ppermute | solution.py:187
  23.7 12.9 %collective-permute-start.8 = (bf16[64,1024]{1,0:T(8,128)(2,1)S(1)}, bf16[64,1024]{1,0:T(8,128)(2,1)S(1)}, u32[]{:S(2)}, u32[]{:S(2)}) collective-permute-start(bf16[64,1024]{1,0:T(8,128)(2,1)S(1)} %get-tuple-element.38), channel_id=1, source_target_pairs={{0,192},{1,65},{2,194},{3,67},{4,196},{5,69},{6,198},{7,71},{8,200... | collective-permute-start | bytes 393224 | tf_op jit(solution)/shard_map/ppermute | solution.py:187
  30.2 16.1 %collective-permute-start.3 = (bf16[48,1024]{1,0:T(8,128)(2,1)S(1)}, bf16[48,1024]{1,0:T(8,128)(2,1)S(1)}, u32[]{:S(2)}, u32[]{:S(2)}) collective-permute-start(bf16[48,1024]{1,0:T(8,128)(2,1)S(1)} %get-tuple-element.32), channel_id=1, source_target_pairs={{0,128},{1,129},{2,130},{3,131},{4,132},{5,133},{6,134},{7,135},{8... | collective-permute-start | bytes 294920 | tf_op jit(solution)/shard_map/ppermute | solution.py:187
  33.9 12.4 %collective-permute-start.4 = (bf16[48,1024]{1,0:T(8,128)(2,1)S(1)}, bf16[48,1024]{1,0:T(8,128)(2,1)S(1)}, u32[]{:S(2)}, u32[]{:S(2)}) collective-permute-start(bf16[48,1024]{1,0:T(8,128)(2,1)S(1)} %get-tuple-element.33), channel_id=1, source_target_pairs={{0,64},{1,193},{2,66},{3,195},{4,68},{5,197},{6,70},{7,199},{8,72}... | collective-permute-start | bytes 294920 | tf_op jit(solution)/shard_map/ppermute | solution.py:187
  35.9 10.3 %collective-permute-start.5 = (bf16[48,1024]{1,0:T(8,128)(2,1)S(1)}, bf16[48,1024]{1,0:T(8,128)(2,1)S(1)}, u32[]{:S(2)}, u32[]{:S(2)}) collective-permute-start(bf16[48,1024]{1,0:T(8,128)(2,1)S(1)} %get-tuple-element.34), channel_id=1, source_target_pairs={{0,192},{1,65},{2,194},{3,67},{4,196},{5,69},{6,198},{7,71},{8,200... | collective-permute-start | bytes 294920 | tf_op jit(solution)/shard_map/ppermute | solution.py:187
  37.2 4.7 %collective-permute-start.9 = (bf16[16,1024]{1,0:T(8,128)(2,1)S(1)}, bf16[16,1024]{1,0:T(8,128)(2,1)S(1)}, u32[]{:S(2)}, u32[]{:S(2)}) collective-permute-start(bf16[16,1024]{1,0:T(8,128)(2,1)S(1)} %get-tuple-element.40), channel_id=1, source_target_pairs={{0,32},{1,33},{2,34},{3,35},{4,36},{5,37},{6,38},{7,39},{8,40},{9,... | collective-permute-start | bytes 98312 | tf_op jit(solution)/shard_map/ppermute | solution.py:187
  39.8 3.4 %collective-permute-start.10 = (bf16[16,1024]{1,0:T(8,128)(2,1)S(1)}, bf16[16,1024]{1,0:T(8,128)(2,1)S(1)}, u32[]{:S(2)}, u32[]{:S(2)}) collective-permute-start(bf16[16,1024]{1,0:T(8,128)(2,1)S(1)} %get-tuple-element.41), channel_id=1, source_target_pairs={{0,16},{1,49},{2,18},{3,51},{4,20},{5,53},{6,22},{7,55},{8,24},{9,... | collective-permute-start | bytes 98312 | tf_op jit(solution)/shard_map/ppermute | solution.py:187
  41.9 4.3 %collective-permute-start.11 = (bf16[16,1024]{1,0:T(8,128)(2,1)S(1)}, bf16[16,1024]{1,0:T(8,128)(2,1)S(1)}, u32[]{:S(2)}, u32[]{:S(2)}) collective-permute-start(bf16[16,1024]{1,0:T(8,128)(2,1)S(1)} %get-tuple-element.42), channel_id=1, source_target_pairs={{0,48},{1,17},{2,50},{3,19},{4,52},{5,21},{6,54},{7,23},{8,56},{9,... | collective-permute-start | bytes 98312 | tf_op jit(solution)/shard_map/ppermute | solution.py:187

commit v3 on v0

v3 whole, which is shorter than its diff:
```python
import functools
import math

import jax
import jax.numpy as jnp
import numpy as np
from jax import lax
from jax.experimental import pallas as pl
from jax.experimental.pallas import tpu as pltpu
from jax.sharding import Mesh
from jax.sharding import PartitionSpec as P

BASE = 5
MODULUS = 1024
ZH, XS, RCV, CORES = 4, 4, 16, 2
RAYS, WIDTH, LOCAL = 512, 1024, 1024
SHARE = RAYS // (ZH * XS)
ROWS = 2 * ZH * SHARE
DEPTH = 2 * LOCAL
VMEM = pl.BlockSpec(memory_space=pltpu.VMEM)
SMEM = pl.BlockSpec(memory_space=pltpu.SMEM)
HBM = pl.BlockSpec(memory_space=pltpu.HBM)
FAR, NEAR, BACK, HERE = (2, 0), (0, 1), (0, -1), (0, 0)
F32, BF16 = jnp.float32, jnp.bfloat16


def fitted(fn, degree):
    points = 0.125 * (1 + np.cos(np.pi * (np.arange(400) + 0.5) / 400))
    series = np.polynomial.chebyshev.Chebyshev.fit(points, fn(np.sqrt(points)), degree, domain=[0, 0.25])
    return [float(a) for a in series.convert(kind=np.polynomial.Polynomial).coef]


HALF_COS = fitted(lambda f: np.cos(np.pi * f), 4)
HALF_SIN = fitted(lambda f: np.sin(np.pi * f) / f, 4)
ROOT_SIN = fitted(lambda f: math.sqrt(2.0) * np.sin(np.pi * f) / f, 4)


def horner(coefs, v):
    total = v * coefs[-1] + coefs[-2]
    for a in coefs[-3::-1]:
        total = total * v + a
    return total


def cosine(turns):
    f = turns - jnp.round(turns)
    t = f * horner(ROOT_SIN, f * f)
    return 1.0 - t * t


def cos_minus_sin(turns):
    f = turns - jnp.round(turns)
    v = f * f
    s = f * horner(HALF_SIN, v)
    twice = s * -2.0
    return twice * s + 1.0, twice * horner(HALF_COS, v)


def iota(shape, axis):
    return lax.broadcasted_iota(jnp.int32, shape, axis)


def ray_columns(ray_ref):
    row = iota((8, RAYS), 0)
    r0, r1 = ray_ref[0:1, :].astype(F32), ray_ref[1:2, :].astype(F32)
    return jnp.where(row < 2, r0, jnp.where(row < 4, r1, jnp.where(row == 4, 1.0, 0.0))).astype(BF16)


def picked(columns, lane_of_row, turn, quarters):
    rows = lane_of_row.shape[0]
    chosen = (iota((rows, RAYS), 1) == lane_of_row).astype(BF16)
    p = lax.dot_general(chosen, columns, (((1,), (1,)), ((), ())), preferred_element_type=F32)
    col = iota((rows, 8), 1)
    p = jnp.where(col < 4, p * turn, p)
    high = p.astype(BF16).astype(F32)
    p = jnp.where((col == 1) | (col == 3), p - high, high)
    return jnp.where(col == 5, quarters, p).astype(BF16)


def grid_rows(grid_ref, shots_ref):
    row = iota((8, LOCAL), 0)
    g = jnp.where(row < 2, grid_ref[0:1, :], jnp.where(row < 4, grid_ref[1:2, :], 0)).astype(F32).astype(BF16)
    twice = (iota((128, 256), 0) == iota((128, 256), 1) // 2).astype(BF16)
    rest = iota((8, 256), 0)
    rest = jnp.where(rest == 4, (iota((8, 256), 1) % 2).astype(F32) * -0.25, jnp.where(rest == 5, 1.0, 0.0))
    for i in range(LOCAL // 128):
        wide = jnp.dot(g[:, i * 128 : (i + 1) * 128], twice, preferred_element_type=F32) + rest
        shots_ref[:, i * 256 : (i + 1) * 256] = wide.astype(BF16)


def chosen_rows(step, place_ref, columns):
    here, wave, turn, first_stride, other_stride = (place_ref[k] for k in (2, 3, 4, 5, 6))
    target = (here + step[0] + step[1] * turn) % 4
    row = iota((ROWS, 1), 0)
    lane = row // (2 * SHARE) * other_stride + target * first_stride + row // 2 % SHARE
    quarters = (row % 2).astype(F32) * 0.25
    return picked(columns, lane, wave.astype(F32) / MODULUS, quarters)


def phase_rows(p, shots_ref, lhs, start, stop):
    for k in range(start, stop, 256):
        lhs[:, k : k + 256] = cosine(jnp.dot(p, shots_ref[:, k : k + 256], preferred_element_type=F32)).astype(BF16)


def first_kernel(place_ref, ray_ref, grid_ref, x_ref, out, data_ref, shots_ref, lhs, total, buf, ray_buf, grid_buf, sems):
    small = [pltpu.make_async_copy(ray_ref, ray_buf, sems.at[8]), pltpu.make_async_copy(grid_ref, grid_buf, sems.at[9])]
    for copy in small:
        copy.start()
    part = LOCAL // 8
    copies = []
    for i in range(8):
        at = pl.ds(i * part, part)
        copies.append(pltpu.make_async_copy(x_ref.at[at], buf.at[at], sems.at[i]))
        copies[-1].start()
    for copy in small:
        copy.wait()
    grid_rows(grid_buf, shots_ref)
    p = chosen_rows(FAR, place_ref, ray_columns(ray_buf))
    phase_rows(p, shots_ref, lhs, 0, DEPTH)
    for i in range(0, 8, 2):
        copies[i].wait()
        copies[i + 1].wait()
        for s in range(i * part, (i + 2) * part, 8):
            data_ref[2 * s : 2 * s + 16] = buf[s : s + 8].reshape(16, WIDTH)
        depth = slice(2 * i * part, 2 * (i + 2) * part)
        for n in range(0, WIDTH, 256):
            r = jnp.dot(lhs[:, depth], data_ref[depth, n : n + 256], preferred_element_type=F32)
            if i > 0:
                r = r + total[:, n : n + 256]
            if i < 6:
                total[:, n : n + 256] = r
            else:
                out[:, n : n + 256] = r.astype(out.dtype)


def first(spot, ray_table, shot_grid, data):
    held = [pltpu.with_memory_space_constraint(a, pltpu.HBM) for a in (ray_table, shot_grid, data)]
    return pl.pallas_call(
        first_kernel,
        out_shape=[jax.ShapeDtypeStruct((n, m), BF16) for n, m in ((ROWS, WIDTH), (DEPTH, WIDTH), (8, DEPTH))],
        in_specs=[SMEM, HBM, HBM, HBM],
        out_specs=[VMEM] * 3,
        scratch_shapes=[
            pltpu.VMEM((ROWS, DEPTH), BF16),
            pltpu.VMEM((ROWS, WIDTH), F32),
            pltpu.VMEM((LOCAL, 2, WIDTH), BF16),
            pltpu.VMEM((2, RAYS), jnp.int32),
            pltpu.VMEM((2, LOCAL), jnp.int32),
            pltpu.SemaphoreType.DMA((10,)),
        ],
        compiler_params=pltpu.CompilerParams(vmem_limit_bytes=20 * 2**20),
        cost_estimate=pl.CostEstimate(flops=2 * ROWS * DEPTH * WIDTH, bytes_accessed=8 * 2**20, transcendentals=0),
        name="encode_first",
    )(spot, *held)


def later_kernel(steps, place_ref, ray_ref, shots_ref, data_ref, *refs):
    outs, lhs = refs[: len(steps)], refs[len(steps) :]
    columns = ray_columns(ray_ref)
    ps = [chosen_rows(step, place_ref, columns) for step in steps]
    phase_rows(ps[0], shots_ref, lhs[0], 0, DEPTH)
    for i, out in enumerate(outs):
        for n in range(4):
            if i + 1 < len(outs):
                phase_rows(ps[i + 1], shots_ref, lhs[i + 1], n * DEPTH // 4, (n + 1) * DEPTH // 4)
            at = slice(n * 256, (n + 1) * 256)
            out[:, at] = jnp.dot(lhs[i][...], data_ref[:, at], preferred_element_type=F32).astype(out.dtype)


def later(steps, dtypes, spot, ray_table, shots, data):
    return pl.pallas_call(
        functools.partial(later_kernel, steps),
        out_shape=[jax.ShapeDtypeStruct((ROWS, WIDTH), dtype) for dtype in dtypes],
        in_specs=[SMEM] + [VMEM] * 3,
        out_specs=[VMEM] * len(steps),
        scratch_shapes=[pltpu.VMEM((ROWS, DEPTH), BF16)] * len(steps),
        compiler_params=pltpu.CompilerParams(vmem_limit_bytes=20 * 2**20),
        cost_estimate=pl.CostEstimate(flops=2 * len(steps) * ROWS * DEPTH * WIDTH, bytes_accessed=8 * 2**20, transcendentals=0),
        name="encode_later",
    )(spot, ray_table, shots, data)


def add_kernel(own, *refs):
    total = own[...]
    for piece in refs[:-1]:
        total = total + piece[...].astype(F32)
    refs[-1][...] = total.astype(BF16)


def add(own, *pieces):
    return pl.pallas_call(
        add_kernel,
        out_shape=jax.ShapeDtypeStruct(own.shape, BF16),
        in_specs=[VMEM] * (1 + len(pieces)),
        out_specs=VMEM,
        compiler_params=pltpu.CompilerParams(vmem_limit_bytes=8 * 2**20),
        name="add",
    )(own, *pieces)


def spread_kernel(place_ref, own, back, near, *outs):
    there, turn = place_ref[7], place_ref[4]
    unit = own.shape[0] // 4
    for step, out in zip((FAR, NEAR, BACK, HERE), outs):
        target = (there + step[0] + step[1] * turn) % 4
        at = pl.ds(pl.multiple_of(target * unit, unit), unit)
        out[...] = (own[at, :] + back[at, :].astype(F32) + near[at, :].astype(F32)).astype(out.dtype)


def spread(spot, own, back, near):
    unit = own.shape[0] // 4
    return pl.pallas_call(
        spread_kernel,
        out_shape=[jax.ShapeDtypeStruct((unit, WIDTH), dtype) for dtype in (BF16, BF16, BF16, F32)],
        in_specs=[SMEM] + [VMEM] * 3,
        out_specs=[VMEM] * 4,
        compiler_params=pltpu.CompilerParams(vmem_limit_bytes=8 * 2**20),
        name="spread",
    )(spot, own, back, near)


def last_kernel(scale, place_ref, ray_ref, rcv_ref, own, far, near, back, out):
    zh, x, wave = place_ref[0], place_ref[1], place_ref[3]
    count = 2 * SHARE
    row8 = iota((8, WIDTH), 0)
    grid = jnp.where(row8 < 2, rcv_ref[0:1, :], jnp.where(row8 < 4, rcv_ref[1:2, :], 0)).astype(F32).astype(BF16)
    row = iota((count, 1), 0)
    lane = zh * (RAYS // ZH) + x * SHARE + row // 2
    p = picked(ray_columns(ray_ref), lane, wave.astype(F32) / MODULUS, 0.0)
    real = row % 2 == 0
    for i in range(0, WIDTH, 256):
        at = slice(i, i + 256)
        c, s = cos_minus_sin(jnp.dot(p, grid[:, at], preferred_element_type=F32))
        total = own[:, at] + far[:, at].astype(F32) + near[:, at].astype(F32) + back[:, at].astype(F32)
        crossed = jnp.where(real, pltpu.roll(total, count - 1, 0), -pltpu.roll(total, 1, 0))
        out[:, at] = (scale * (total * c + crossed * s)).astype(BF16)


def last(scale, spot, ray_table, receiver_grid, *pieces):
    return pl.pallas_call(
        functools.partial(last_kernel, scale),
        out_shape=jax.ShapeDtypeStruct((2 * SHARE, WIDTH), BF16),
        in_specs=[SMEM] + [VMEM] * 6,
        out_specs=VMEM,
        compiler_params=pltpu.CompilerParams(vmem_limit_bytes=8 * 2**20),
        name="last",
    )(spot, ray_table, receiver_grid, *pieces)


def send(value, leg, step):
    pairs = []
    for index in range(ZH * XS * RCV):
        zh, x, rcv = index // (XS * RCV), index // RCV % XS, index % RCV
        move = step[0] + step[1] * (1 - rcv // (RCV // 2) * 2)
        if (rcv % CORES == 0) == (leg == 0):
            x = (x + move) % XS
        else:
            zh = (zh + move) % ZH
        pairs.append((index, (zh * XS + x) * RCV + rcv))
    return lax.ppermute(value, ("z_hi", "x", "rcv"), pairs)


def on_device(spectra, shot_grid, ray_table, receiver_grid):
    scale = 1.0 / math.sqrt(LOCAL * ZH * XS)
    zh, x, rcv = (lax.axis_index(name) for name in ("z_hi", "x", "rcv"))
    first_x = rcv % CORES == 0
    turn = 1 - rcv // (RCV // 2) * 2
    along_x, along_z = SHARE, RAYS // ZH
    spot = [zh, x, jnp.where(first_x, x, zh), BASE + rcv, turn]
    spot += [jnp.where(first_x, along_x, along_z), jnp.where(first_x, along_z, along_x), jnp.where(first_x, zh, x)]
    spot = jnp.stack(spot).astype(jnp.int32)
    far, data, shots = first(spot, ray_table, shot_grid, spectra.reshape(LOCAL, 2, WIDTH))
    relayed = send(far, 0, NEAR)
    back, near = later([BACK, NEAR], [BF16, F32], spot, ray_table, shots, data)
    from_back = send(back, 0, BACK)
    from_near = send(add(near, relayed), 0, NEAR)
    shots, back = lax.optimization_barrier((shots, back))
    (here,) = later([HERE], [F32], spot, ray_table, shots, data)
    far, near, back, here = spread(spot, here, from_back, from_near)
    pieces = [send(far, 1, FAR), send(near, 1, NEAR), send(back, 1, BACK)]
    turned = last(scale, spot, ray_table, receiver_grid, here, *pieces)
    return lax.all_to_all(turned.reshape(SHARE, 1, 2, WIDTH), "rcv", split_axis=0, concat_axis=1, tiled=True)


def solution(mesh):
    split = Mesh(mesh.devices.reshape(ZH, XS, RCV), ("z_hi", "x", "rcv"))
    in_specs = (P("rcv", ("z_hi", "x"), None, None), P(None, ("z_hi", "x")), P(), P())
    out_specs = P(("z_hi", "x", "rcv"), None, None, None)
    return jax.shard_map(on_device, mesh=split, in_specs=in_specs, out_specs=out_specs, check_vma=False)
```

time: 279 us -> 55.9 us (0.20)
  waiting for transfers between devices: 220 us -> 8.1 us
  starting transfers between devices: 0.01 us -> 19 us
  other arithmetic: 14.5 us -> 0 us
  Pallas kernels: 0 us -> 13.9 us
  between operations: 13.4 us -> 0.07 us
  local copies, waits for them, and re-layouts: 8.76 us -> 0.89 us
  matrix products: 6.29 us -> 0 us
  blocking collectives: 16.7 us -> 13.9 us
    psum x1 -> x0, waiting for transfers between devices: 219 us -> none  [on_device(): summed = lax.psum(jnp.stack(pieces, 1), 'shot')]
    ppermute x0 -> x6, starting transfers between devices: none -> 19 us  [send(): return lax.ppermute(value, ('z_hi', 'x', 'rcv'), pairs)]
    another operation x5 -> x0, other arithmetic: 14.5 us -> none
    pallas_call x0 -> x6, Pallas kernels: none -> 13.9 us  [the longest x2 7.58 us: later(): pl.pallas_call(functools.partial(later_kernel, steps), out_shape=[jax.Sha...]
    ppermute x0 -> x6, waiting for transfers between devices: none -> 8.1 us  [send(): return lax.ppermute(value, ('z_hi', 'x', 'rcv'), pairs)]
    dot_general x1 -> x0, matrix products: 6.29 us -> none  [on_device(): jnp.dot(phases, local_data[offset], preferred_element_type=jnp.float32)]
    unnamed x3 -> x4, local copies, waits for them, and re-layouts: 5.56 us -> 0.01 us
  transfers between devices with their start and end apart: 1 -> 6, of which waited for: 1 -> 4; matrix products, arithmetic and copies ran while one was open for 0% -> 0% of each run, Pallas kernels for 0% -> 14%
where the time goes in v3:
time: 55.9 us; the launch traced here: 55.8 us
  starting transfers between devices  19 us (34%)
  Pallas kernels  13.9 us (25%)
  blocking collectives  13.9 us (25%)
  waiting for transfers between devices  8.1 us (14%)
  local copies, waits for them, and re-layouts  0.89 us (2%)
    ppermute x6, starting transfers between devices, send(): return lax.ppermute(value, ('z_hi', 'x', 'rcv'), pairs)  19 us
    all_to_all x1, blocking collectives, on_device(): lax.all_to_all(turned.reshape(SHARE, 1, 2, WIDTH), 'rcv', split_axis=0, c...  13.9 us
    ppermute x6, waiting for transfers between devices, send(): return lax.ppermute(value, ('z_hi', 'x', 'rcv'), pairs)  8.1 us
    pallas_call x2, Pallas kernels, later(): pl.pallas_call(functools.partial(later_kernel, steps), out_shape=[jax.Sha...  7.58 us
    pallas_call x1, Pallas kernels, first(): pl.pallas_call(first_kernel, out_shape=[jax.ShapeDtypeStruct((n, m), BF16...  4.39 us
    pallas_call x1, Pallas kernels, last(): pl.pallas_call(functools.partial(last_kernel, scale), out_shape=jax.Shape...  1.13 us
  transfers between devices with their start and end apart: 6, of which 4 were waited for; matrix products, arithmetic and copies ran while one was open for 0% of the time, Pallas kernels for 14%

profile of v3, /device:TPU:1, one launch (start us, length us, event | category | flops | bytes accessed | tf_op | source)
XLA Modules:
  0.0 55.8 jit_solution(1299669958138032062)
XLA Ops:
  0.0 0.0 copy-start
  0.0 0.1 stack.35.place_ref
  0.1 4.4 %encode_first.1 = (bf16[256,1024]{1,0:T(8,128)(2,1)S(1)}, bf16[2048,1024]{1,0:T(8,128)(2,1)S(1)}, bf16[8,2048]{1,0:T(8,128)(2,1)S(1)}) custom-call(s32[8]{0:T(128)S(1)} %stack.35.place_ref, s32[2,512]{1,0:T(2,128)} %ray_ref.7, s32[2,1024]{1,0:T(2,128)} %grid_ref.1, bf16[1024,2,1024]{2,1,0:T(2,128)(2,1)} %bitcast.15), custom_call_target="tpu_custom_call" | custom-call | flops 1073741824 | bytes 8388608 | tf_op jit(solution)/shard_map/encode_first/pallas_call | solution.py:138
  4.5 3.9 %collective-permute-start.1 = (bf16[256,1024]{1,0:T(8,128)(2,1)S(1)}, bf16[256,1024]{1,0:T(8,128)(2,1)S(1)}, u32[]{:S(2)}, u32[]{:S(2)}) collective-permute-start(bf16[256,1024]{1,0:T(8,128)(2,1)S(1)} %get-tuple-element.20), channel_id=1, source_target_pairs={{0,16},{1,65},{2,18},{3,67},{4,20},{5,69},{6,22},{7,71},{8,56},{9,... | collective-permute-start | bytes 1572872 | tf_op jit(solution)/shard_map/ppermute | solution.py:260
  8.4 0.0 copy-done
  8.4 4.6 %encode_later.2 = (bf16[256,1024]{1,0:T(8,128)(2,1)S(1)}, f32[256,1024]{1,0:T(8,128)S(1)}) custom-call(s32[8]{0:T(128)S(1)} %stack.35.place_ref, s32[2,512]{1,0:T(2,128)S(1)} %copy-done, bf16[8,2048]{1,0:T(8,128)(2,1)S(1)} %get-tuple-element.18.shots_ref, bf16[2048,1024]{1,0:T(8,128)(2,1)S(1)} %get-tuple-element.16.data_ref), custom_call_target="tpu_custom_call" | custom-call | flops 2147483648 | bytes 8388608 | tf_op jit(solution)/shard_map/encode_later/pallas_call | solution.py:171
  13.0 3.1 %collective-permute-start = (bf16[256,1024]{1,0:T(8,128)(2,1)S(1)}, bf16[256,1024]{1,0:T(8,128)(2,1)S(1)}, u32[]{:S(2)}, u32[]{:S(2)}) collective-permute-start(bf16[256,1024]{1,0:T(8,128)(2,1)S(1)} %get-tuple-element.17), channel_id=1, source_target_pairs={{0,48},{1,193},{2,50},{3,195},{4,52},{5,197},{6,54},{7,199},{8,24}... | collective-permute-start | bytes 1572872 | tf_op jit(solution)/shard_map/ppermute | solution.py:260
  16.1 1.9 %collective-permute-done.1.refs_0_ = bf16[256,1024]{1,0:T(8,128)(2,1)S(1)} collective-permute-done((bf16[256,1024]{1,0:T(8,128)(2,1)S(1)}, bf16[256,1024]{1,0:T(8,128)(2,1)S(1)}, u32[]{:S(2)}, u32[]{:S(2)}) %collective-permute-start.1) | collective-permute-done | bytes 524320 | tf_op jit(solution)/shard_map/ppermute | solution.py:260
  18.0 0.1 add.7
  18.1 0.0 copy-start.1
  18.1 6.4 %collective-permute-start.2 = (bf16[256,1024]{1,0:T(8,128)(2,1)S(1)}, bf16[256,1024]{1,0:T(8,128)(2,1)S(1)}, u32[]{:S(2)}, u32[]{:S(2)}) collective-permute-start(bf16[256,1024]{1,0:T(8,128)(2,1)S(1)} %add.7), channel_id=1, source_target_pairs={{0,16},{1,65},{2,18},{3,67},{4,20},{5,69},{6,22},{7,71},{8,56},{9,... | collective-permute-start | bytes 1572872 | tf_op jit(solution)/shard_map/ppermute | solution.py:260
  24.5 3.0 %encode_later.3.own = f32[256,1024]{1,0:T(8,128)S(1)} custom-call(s32[8]{0:T(128)S(1)} %stack.35.place_ref, s32[2,512]{1,0:T(2,128)S(1)} %copy-done, bf16[8,2048]{1,0:T(8,128)(2,1)S(1)} %get-tuple-element.18.shots_ref, bf16[2048,1024]{1,0:T(8,128)(2,1)S(1)} %get-tuple-element.16.data_ref), custom_call_target="tpu_custom_call" | custom-call | flops 1073741824 | bytes 8388608 | tf_op jit(solution)/shard_map/encode_later/pallas_call | solution.py:171
  27.5 0.0 collective-permute-done.back
  27.5 3.9 %collective-permute-done.2.near = bf16[256,1024]{1,0:T(8,128)(2,1)S(1)} collective-permute-done((bf16[256,1024]{1,0:T(8,128)(2,1)S(1)}, bf16[256,1024]{1,0:T(8,128)(2,1)S(1)}, u32[]{:S(2)}, u32[]{:S(2)}) %collective-permute-start.2) | collective-permute-done | bytes 524320 | tf_op jit(solution)/shard_map/ppermute | solution.py:260
  31.4 0.7 %spread.1 = (bf16[64,1024]{1,0:T(8,128)(2,1)S(1)}, bf16[64,1024]{1,0:T(8,128)(2,1)S(1)}, bf16[64,1024]{1,0:T(8,128)(2,1)S(1)}, f32[64,1024]{1,0:T(8,128)S(1)}) custom-call(s32[8]{0:T(128)S(1)} %stack.35.place_ref, f32[256,1024]{1,0:T(8,128)S(1)} %encode_later.3.own, bf16[256,1024]{1,0:T(8,128)(2,1)S(1)} %collective-permute-done.back, ...), custom_call_target="tpu_custom_call" | custom-call | tf_op jit(solution)/shard_map/spread/pallas_call | solution.py:212
  32.1 2.8 %collective-permute-start.3 = (bf16[64,1024]{1,0:T(8,128)(2,1)S(1)}, bf16[64,1024]{1,0:T(8,128)(2,1)S(1)}, u32[]{:S(2)}, u32[]{:S(2)}) collective-permute-start(bf16[64,1024]{1,0:T(8,128)(2,1)S(1)} %get-tuple-element.22), channel_id=1, source_target_pairs={{0,128},{1,33},{2,130},{3,35},{4,132},{5,37},{6,134},{7,39},{8,136... | collective-permute-start | bytes 393224 | tf_op jit(solution)/shard_map/ppermute | solution.py:260
  34.9 0.3 collective-permute-start.4
  35.2 2.4 %collective-permute-start.5 = (bf16[64,1024]{1,0:T(8,128)(2,1)S(1)}, bf16[64,1024]{1,0:T(8,128)(2,1)S(1)}, u32[]{:S(2)}, u32[]{:S(2)}) collective-permute-start(bf16[64,1024]{1,0:T(8,128)(2,1)S(1)} %get-tuple-element.24), channel_id=1, source_target_pairs={{0,192},{1,49},{2,194},{3,51},{4,196},{5,53},{6,198},{7,55},{8,72}... | collective-permute-start | bytes 393224 | tf_op jit(solution)/shard_map/ppermute | solution.py:260
  37.6 0.2 collective-permute-done.3.far
  37.8 2.2 %collective-permute-done.4.near = bf16[64,1024]{1,0:T(8,128)(2,1)S(1)} collective-permute-done((bf16[64,1024]{1,0:T(8,128)(2,1)S(1)}, bf16[64,1024]{1,0:T(8,128)(2,1)S(1)}, u32[]{:S(2)}, u32[]{:S(2)}) %collective-permute-start.4) | collective-permute-done | bytes 131104 | tf_op jit(solution)/shard_map/ppermute | solution.py:260
  40.0 0.0 collective-permute-done.5.back
  40.0 0.0 copy-done.1
  40.0 1.1 %last.1 = bf16[64,1024]{1,0:T(8,128)(2,1)S(1)} custom-call(s32[8]{0:T(128)S(1)} %stack.35.place_ref, s32[2,512]{1,0:T(2,128)S(1)} %copy-done, s32[2,1024]{1,0:T(2,128)S(1)} %copy-done.1, f32[64,1024]{1,0:T(8,128)S(1)} %get-tuple-element.21.own, bf16[64,1024]{1,0:T(8,128)(2,1)S(1)} %collective-permute-done.3.far, ...), custom_call_target="tpu_custom_call" | custom-call | tf_op jit(solution)/shard_map/last/pallas_call | solution.py:240
  41.1 0.1 reshape.7
  41.2 13.9 %all_to_all.18 = bf16[32,1,2,1024]{3,2,1,0:T(2,128)(2,1)S(1)} all-to-all(bf16[32,1,2,1024]{3,2,1,0:T(2,128)(2,1)S(1)} %bitcast.16), channel_id=1, replica_groups=mesh['z_hi'=4,'x'=4,'rcv'=16] {'rcv'}, dimensions={0} | all-to-all | bytes 262144 | tf_op jit(solution)/shard_map/all_to_all | solution.py:282
  55.1 0.7 %copy.7 = bf16[2,16,2,1024]{3,2,1,0:T(2,128)(2,1)} copy(bf16[2,16,2,1024]{3,2,0,1:T(2,128)(2,1)S(1)} %bitcast.17) | data formatting | bytes 262144 | tf_op jit(solution)/shard_map/all_to_all | solution.py:282
Async XLA Ops:
  0.0 8.4 %copy-start = (s32[2,512]{1,0:T(2,128)S(1)}, s32[2,512]{1,0:T(2,128)}, u32[]{:S(2)}) copy-start(s32[2,512]{1,0:T(2,128)} %ray_ref.7) | copy-start | bytes 12292
  4.5 13.5 %collective-permute-start.1 = (bf16[256,1024]{1,0:T(8,128)(2,1)S(1)}, bf16[256,1024]{1,0:T(8,128)(2,1)S(1)}, u32[]{:S(2)}, u32[]{:S(2)}) collective-permute-start(bf16[256,1024]{1,0:T(8,128)(2,1)S(1)} %get-tuple-element.20), channel_id=1, source_target_pairs={{0,16},{1,65},{2,18},{3,67},{4,20},{5,69},{6,22},{7,71},{8,56},{9,... | collective-permute-start | bytes 1572872 | tf_op jit(solution)/shard_map/ppermute | solution.py:260
  13.0 14.6 %collective-permute-start = (bf16[256,1024]{1,0:T(8,128)(2,1)S(1)}, bf16[256,1024]{1,0:T(8,128)(2,1)S(1)}, u32[]{:S(2)}, u32[]{:S(2)}) collective-permute-start(bf16[256,1024]{1,0:T(8,128)(2,1)S(1)} %get-tuple-element.17), channel_id=1, source_target_pairs={{0,48},{1,193},{2,50},{3,195},{4,52},{5,197},{6,54},{7,199},{8,24}... | collective-permute-start | bytes 1572872 | tf_op jit(solution)/shard_map/ppermute | solution.py:260
  18.1 21.9 %copy-start.1 = (s32[2,1024]{1,0:T(2,128)S(1)}, s32[2,1024]{1,0:T(2,128)}, u32[]{:S(2)}) copy-start(s32[2,1024]{1,0:T(2,128)} %rcv_ref.1) | copy-start | bytes 24580
  18.1 13.3 %collective-permute-start.2 = (bf16[256,1024]{1,0:T(8,128)(2,1)S(1)}, bf16[256,1024]{1,0:T(8,128)(2,1)S(1)}, u32[]{:S(2)}, u32[]{:S(2)}) collective-permute-start(bf16[256,1024]{1,0:T(8,128)(2,1)S(1)} %add.7), channel_id=1, source_target_pairs={{0,16},{1,65},{2,18},{3,67},{4,20},{5,69},{6,22},{7,71},{8,56},{9,... | collective-permute-start | bytes 1572872 | tf_op jit(solution)/shard_map/ppermute | solution.py:260
  32.1 5.7 %collective-permute-start.3 = (bf16[64,1024]{1,0:T(8,128)(2,1)S(1)}, bf16[64,1024]{1,0:T(8,128)(2,1)S(1)}, u32[]{:S(2)}, u32[]{:S(2)}) collective-permute-start(bf16[64,1024]{1,0:T(8,128)(2,1)S(1)} %get-tuple-element.22), channel_id=1, source_target_pairs={{0,128},{1,33},{2,130},{3,35},{4,132},{5,37},{6,134},{7,39},{8,136... | collective-permute-start | bytes 393224 | tf_op jit(solution)/shard_map/ppermute | solution.py:260
  34.9 5.0 %collective-permute-start.4 = (bf16[64,1024]{1,0:T(8,128)(2,1)S(1)}, bf16[64,1024]{1,0:T(8,128)(2,1)S(1)}, u32[]{:S(2)}, u32[]{:S(2)}) collective-permute-start(bf16[64,1024]{1,0:T(8,128)(2,1)S(1)} %get-tuple-element.23), channel_id=1, source_target_pairs={{0,64},{1,17},{2,66},{3,19},{4,68},{5,21},{6,70},{7,23},{8,200},{9... | collective-permute-start | bytes 393224 | tf_op jit(solution)/shard_map/ppermute | solution.py:260
  35.2 4.7 %collective-permute-start.5 = (bf16[64,1024]{1,0:T(8,128)(2,1)S(1)}, bf16[64,1024]{1,0:T(8,128)(2,1)S(1)}, u32[]{:S(2)}, u32[]{:S(2)}) collective-permute-start(bf16[64,1024]{1,0:T(8,128)(2,1)S(1)} %get-tuple-element.24), channel_id=1, source_target_pairs={{0,192},{1,49},{2,194},{3,51},{4,196},{5,53},{6,198},{7,55},{8,72}... | collective-permute-start | bytes 393224 | tf_op jit(solution)/shard_map/ppermute | solution.py:260

commit v4 on v3

--- a/solution.py
+++ b/solution.py
@@ -21,6 +21,7 @@
 SMEM = pl.BlockSpec(memory_space=pltpu.SMEM)
 HBM = pl.BlockSpec(memory_space=pltpu.HBM)
 FAR, NEAR, BACK, HERE = (2, 0), (0, 1), (0, -1), (0, 0)
+SCALE = 1.0 / math.sqrt(LOCAL * ZH * XS)
 F32, BF16 = jnp.float32, jnp.bfloat16
 
 
@@ -89,10 +90,12 @@
 
 
 def chosen_rows(step, place_ref, columns):
-    here, wave, turn, first_stride, other_stride = (place_ref[k] for k in (2, 3, 4, 5, 6))
+    here, wave, turn, first_stride, other_stride, there = (place_ref[k] for k in (2, 3, 4, 5, 6, 7))
     target = (here + step[0] + step[1] * turn) % 4
     row = iota((ROWS, 1), 0)
-    lane = row // (2 * SHARE) * other_stride + target * first_stride + row // 2 % SHARE
+    piece = row // (2 * SHARE)
+    move = jnp.where(piece == 0, FAR[0], jnp.where(piece == 1, turn, jnp.where(piece == 2, -turn, 0)))
+    lane = (there + move + 4) % 4 * other_stride + target * first_stride + row // 2 % SHARE
     quarters = (row % 2).astype(F32) * 0.25
     return picked(columns, lane, wave.astype(F32) / MODULUS, quarters)
 
@@ -116,21 +119,22 @@
         copy.wait()
     grid_rows(grid_buf, shots_ref)
     p = chosen_rows(FAR, place_ref, ray_columns(ray_buf))
-    phase_rows(p, shots_ref, lhs, 0, DEPTH)
-    for i in range(0, 8, 2):
-        copies[i].wait()
-        copies[i + 1].wait()
-        for s in range(i * part, (i + 2) * part, 8):
-            data_ref[2 * s : 2 * s + 16] = buf[s : s + 8].reshape(16, WIDTH)
-        depth = slice(2 * i * part, 2 * (i + 2) * part)
+    half = DEPTH // 2
+    phase_rows(p, shots_ref, lhs, 0, half)
+    for step in range(2):
+        for i in range(4 * step, 4 * step + 4):
+            copies[i].wait()
+            for s in range(i * part, (i + 1) * part, 8):
+                data_ref[2 * s : 2 * s + 16] = buf[s : s + 8].reshape(16, WIDTH)
+        depth = slice(step * half, (step + 1) * half)
         for n in range(0, WIDTH, 256):
+            if step == 0:
+                phase_rows(p, shots_ref, lhs, half + n, half + n + 256)
             r = jnp.dot(lhs[:, depth], data_ref[depth, n : n + 256], preferred_element_type=F32)
-            if i > 0:
-                r = r + total[:, n : n + 256]
-            if i < 6:
+            if step == 0:
                 total[:, n : n + 256] = r
             else:
-                out[:, n : n + 256] = r.astype(out.dtype)
+                out[:, n : n + 256] = (r + total[:, n : n + 256]).astype(out.dtype)
 
 
 def first(spot, ray_table, shot_grid, data):
@@ -167,17 +171,34 @@
             out[:, at] = jnp.dot(lhs[i][...], data_ref[:, at], preferred_element_type=F32).astype(out.dtype)
 
 
-def later(steps, dtypes, spot, ray_table, shots, data):
-    return pl.pallas_call(
-        functools.partial(later_kernel, steps),
-        out_shape=[jax.ShapeDtypeStruct((ROWS, WIDTH), dtype) for dtype in dtypes],
-        in_specs=[SMEM] + [VMEM] * 3,
-        out_specs=[VMEM] * len(steps),
+def own_kernel(place_ref, ray_ref, shots_ref, data_ref, rcv_ref, out, cos_ref, sin_ref, lhs):
+    later_kernel((HERE,), place_ref, ray_ref, shots_ref, data_ref, out, lhs)
+    row = iota((2 * SHARE, 1), 0)
+    row8 = iota((8, WIDTH), 0)
+    grid = jnp.where(row8 < 2, rcv_ref[0:1, :], jnp.where(row8 < 4, rcv_ref[1:2, :], 0)).astype(F32).astype(BF16)
+    lane = place_ref[0] * (RAYS // ZH) + place_ref[1] * SHARE + row // 2
+    p = picked(ray_columns(ray_ref), lane, place_ref[3].astype(F32) / MODULUS, 0.0)
+    for i in range(0, WIDTH, 256):
+        at = slice(i, i + 256)
+        c, s = cos_minus_sin(jnp.dot(p, grid[:, at], preferred_element_type=F32))
+        cos_ref[:, at] = SCALE * c
+        sin_ref[:, at] = jnp.where(row % 2 == 0, SCALE * s, -SCALE * s)
+
+
+def later(steps, dtypes, spot, ray_table, shots, data, *more):
+    shapes = [jax.ShapeDtypeStruct((ROWS, WIDTH), dtype) for dtype in dtypes]
+    if more:
+        shapes += [jax.ShapeDtypeStruct((2 * SHARE, WIDTH), F32)] * 2
+    return pl.pallas_call(
+        own_kernel if more else functools.partial(later_kernel, steps),
+        out_shape=shapes,
+        in_specs=[SMEM] + [VMEM] * (3 + len(more)),
+        out_specs=[VMEM] * len(shapes),
         scratch_shapes=[pltpu.VMEM((ROWS, DEPTH), BF16)] * len(steps),
         compiler_params=pltpu.CompilerParams(vmem_limit_bytes=20 * 2**20),
         cost_estimate=pl.CostEstimate(flops=2 * len(steps) * ROWS * DEPTH * WIDTH, bytes_accessed=8 * 2**20, transcendentals=0),
         name="encode_later",
-    )(spot, ray_table, shots, data)
+    )(spot, ray_table, shots, data, *more)
 
 
 def add_kernel(own, *refs):
@@ -198,53 +219,44 @@
     )(own, *pieces)
 
 
-def spread_kernel(place_ref, own, back, near, *outs):
-    there, turn = place_ref[7], place_ref[4]
+def spread_kernel(own, back, near, *outs):
     unit = own.shape[0] // 4
-    for step, out in zip((FAR, NEAR, BACK, HERE), outs):
-        target = (there + step[0] + step[1] * turn) % 4
-        at = pl.ds(pl.multiple_of(target * unit, unit), unit)
+    for k, out in enumerate(outs):
+        at = slice(k * unit, (k + 1) * unit)
         out[...] = (own[at, :] + back[at, :].astype(F32) + near[at, :].astype(F32)).astype(out.dtype)
 
 
-def spread(spot, own, back, near):
+def spread(own, back, near):
     unit = own.shape[0] // 4
     return pl.pallas_call(
         spread_kernel,
         out_shape=[jax.ShapeDtypeStruct((unit, WIDTH), dtype) for dtype in (BF16, BF16, BF16, F32)],
-        in_specs=[SMEM] + [VMEM] * 3,
+        in_specs=[VMEM] * 3,
         out_specs=[VMEM] * 4,
         compiler_params=pltpu.CompilerParams(vmem_limit_bytes=8 * 2**20),
         name="spread",
-    )(spot, own, back, near)
-
-
-def last_kernel(scale, place_ref, ray_ref, rcv_ref, own, far, near, back, out):
-    zh, x, wave = place_ref[0], place_ref[1], place_ref[3]
-    count = 2 * SHARE
-    row8 = iota((8, WIDTH), 0)
-    grid = jnp.where(row8 < 2, rcv_ref[0:1, :], jnp.where(row8 < 4, rcv_ref[1:2, :], 0)).astype(F32).astype(BF16)
-    row = iota((count, 1), 0)
-    lane = zh * (RAYS // ZH) + x * SHARE + row // 2
-    p = picked(ray_columns(ray_ref), lane, wave.astype(F32) / MODULUS, 0.0)
-    real = row % 2 == 0
+    )(own, back, near)
+
+
+def last_kernel(own, far, near, back, cos_ref, sin_ref, out):
+    count = own.shape[0]
+    real = iota((count, 1), 0) % 2 == 0
     for i in range(0, WIDTH, 256):
         at = slice(i, i + 256)
-        c, s = cos_minus_sin(jnp.dot(p, grid[:, at], preferred_element_type=F32))
         total = own[:, at] + far[:, at].astype(F32) + near[:, at].astype(F32) + back[:, at].astype(F32)
-        crossed = jnp.where(real, pltpu.roll(total, count - 1, 0), -pltpu.roll(total, 1, 0))
-        out[:, at] = (scale * (total * c + crossed * s)).astype(BF16)
-
-
-def last(scale, spot, ray_table, receiver_grid, *pieces):
-    return pl.pallas_call(
-        functools.partial(last_kernel, scale),
+        crossed = jnp.where(real, pltpu.roll(total, count - 1, 0), pltpu.roll(total, 1, 0))
+        out[:, at] = (total * cos_ref[:, at] + crossed * sin_ref[:, at]).astype(BF16)
+
+
+def last(*args):
+    return pl.pallas_call(
+        last_kernel,
         out_shape=jax.ShapeDtypeStruct((2 * SHARE, WIDTH), BF16),
-        in_specs=[SMEM] + [VMEM] * 6,
+        in_specs=[VMEM] * 6,
         out_specs=VMEM,
         compiler_params=pltpu.CompilerParams(vmem_limit_bytes=8 * 2**20),
         name="last",
-    )(spot, ray_table, receiver_grid, *pieces)
+    )(*args)
 
 
 def send(value, leg, step):
@@ -261,7 +273,6 @@
 
 
 def on_device(spectra, shot_grid, ray_table, receiver_grid):
-    scale = 1.0 / math.sqrt(LOCAL * ZH * XS)
     zh, x, rcv = (lax.axis_index(name) for name in ("z_hi", "x", "rcv"))
     first_x = rcv % CORES == 0
     turn = 1 - rcv // (RCV // 2) * 2
@@ -275,10 +286,10 @@
     from_back = send(back, 0, BACK)
     from_near = send(add(near, relayed), 0, NEAR)
     shots, back = lax.optimization_barrier((shots, back))
-    (here,) = later([HERE], [F32], spot, ray_table, shots, data)
-    far, near, back, here = spread(spot, here, from_back, from_near)
+    here, cosines, sines = later([HERE], [F32], spot, ray_table, shots, data, receiver_grid)
+    far, near, back, here = spread(here, from_back, from_near)
     pieces = [send(far, 1, FAR), send(near, 1, NEAR), send(back, 1, BACK)]
-    turned = last(scale, spot, ray_table, receiver_grid, here, *pieces)
+    turned = last(here, *pieces, cosines, sines)
     return lax.all_to_all(turned.reshape(SHARE, 1, 2, WIDTH), "rcv", split_axis=0, concat_axis=1, tiled=True)
 
 

time: 55.9 us -> 54.9 us (0.982)
  Pallas kernels: 13.9 us -> 12.6 us
  blocking collectives: 13.9 us -> 14.5 us
    pallas_call x3, Pallas kernels: 8.7 us -> 7.97 us  [the longest x2 7.83 us: later(): pl.pallas_call(own_kernel if more else functools.partial(later_kernel, st...]
    all_to_all x1, blocking collectives: 13.9 us -> 14.5 us  [on_device(): lax.all_to_all(turned.reshape(SHARE, 1, 2, WIDTH), 'rcv', split_axis=0, c...]
where the time goes in v4:
time: 54.9 us; the launch traced here: 54.8 us
  starting transfers between devices  19 us (35%)
  blocking collectives  14.5 us (26%)
  Pallas kernels  12.6 us (23%)
  waiting for transfers between devices  7.76 us (14%)
  local copies, waits for them, and re-layouts  0.89 us (2%)
    ppermute x6, starting transfers between devices, send(): return lax.ppermute(value, ('z_hi', 'x', 'rcv'), pairs)  19 us
    all_to_all x1, blocking collectives, on_device(): lax.all_to_all(turned.reshape(SHARE, 1, 2, WIDTH), 'rcv', split_axis=0, c...  14.5 us
    pallas_call x2, Pallas kernels, later(): pl.pallas_call(own_kernel if more else functools.partial(later_kernel, st...  7.83 us
    ppermute x6, waiting for transfers between devices, send(): return lax.ppermute(value, ('z_hi', 'x', 'rcv'), pairs)  7.76 us
    pallas_call x1, Pallas kernels, first(): pl.pallas_call(first_kernel, out_shape=[jax.ShapeDtypeStruct((n, m), BF16...  4.34 us
  transfers between devices with their start and end apart: 6, of which 4 were waited for; matrix products, arithmetic and copies ran while one was open for 0% of the time, Pallas kernels for 14%

profile of v4, /device:TPU:1, one launch (start us, length us, event | category | flops | bytes accessed | tf_op | source)
XLA Modules:
  0.0 54.8 jit_solution(599104704434284843)
XLA Ops:
  0.0 0.0 copy-start
  0.0 0.1 stack.35.place_ref
  0.1 4.3 %encode_first.1 = (bf16[256,1024]{1,0:T(8,128)(2,1)S(1)}, bf16[2048,1024]{1,0:T(8,128)(2,1)S(1)}, bf16[8,2048]{1,0:T(8,128)(2,1)S(1)}) custom-call(s32[8]{0:T(128)S(1)} %stack.35.place_ref, s32[2,512]{1,0:T(2,128)} %ray_ref.5, s32[2,1024]{1,0:T(2,128)} %grid_ref.1, bf16[1024,2,1024]{2,1,0:T(2,128)(2,1)} %bitcast.15), custom_call_target="tpu_custom_call" | custom-call | flops 1073741824 | bytes 8388608 | tf_op jit(solution)/shard_map/encode_first/pallas_call | solution.py:142
  4.4 3.9 %collective-permute-start.1 = (bf16[256,1024]{1,0:T(8,128)(2,1)S(1)}, bf16[256,1024]{1,0:T(8,128)(2,1)S(1)}, u32[]{:S(2)}, u32[]{:S(2)}) collective-permute-start(bf16[256,1024]{1,0:T(8,128)(2,1)S(1)} %get-tuple-element.24), channel_id=1, source_target_pairs={{0,16},{1,65},{2,18},{3,67},{4,20},{5,69},{6,22},{7,71},{8,56},{9,... | collective-permute-start | bytes 1572872 | tf_op jit(solution)/shard_map/ppermute | solution.py:272
  8.3 0.0 copy-done
  8.3 0.0 copy-start.1
  8.3 4.5 %encode_later.2 = (bf16[256,1024]{1,0:T(8,128)(2,1)S(1)}, f32[256,1024]{1,0:T(8,128)S(1)}) custom-call(s32[8]{0:T(128)S(1)} %stack.35.place_ref, s32[2,512]{1,0:T(2,128)S(1)} %copy-done, bf16[8,2048]{1,0:T(8,128)(2,1)S(1)} %get-tuple-element.21.shots_ref, bf16[2048,1024]{1,0:T(8,128)(2,1)S(1)} %get-tuple-element.19.data_ref), custom_call_target="tpu_custom_call" | custom-call | flops 2147483648 | bytes 8388608 | tf_op jit(solution)/shard_map/encode_later/pallas_call | solution.py:192
  12.8 3.1 %collective-permute-start = (bf16[256,1024]{1,0:T(8,128)(2,1)S(1)}, bf16[256,1024]{1,0:T(8,128)(2,1)S(1)}, u32[]{:S(2)}, u32[]{:S(2)}) collective-permute-start(bf16[256,1024]{1,0:T(8,128)(2,1)S(1)} %get-tuple-element.20), channel_id=1, source_target_pairs={{0,48},{1,193},{2,50},{3,195},{4,52},{5,197},{6,54},{7,199},{8,24}... | collective-permute-start | bytes 1572872 | tf_op jit(solution)/shard_map/ppermute | solution.py:272
  16.0 2.0 %collective-permute-done.1.refs_0_ = bf16[256,1024]{1,0:T(8,128)(2,1)S(1)} collective-permute-done((bf16[256,1024]{1,0:T(8,128)(2,1)S(1)}, bf16[256,1024]{1,0:T(8,128)(2,1)S(1)}, u32[]{:S(2)}, u32[]{:S(2)}) %collective-permute-start.1) | collective-permute-done | bytes 524320 | tf_op jit(solution)/shard_map/ppermute | solution.py:272
  17.9 0.1 add.7
  18.0 6.4 %collective-permute-start.2 = (bf16[256,1024]{1,0:T(8,128)(2,1)S(1)}, bf16[256,1024]{1,0:T(8,128)(2,1)S(1)}, u32[]{:S(2)}, u32[]{:S(2)}) collective-permute-start(bf16[256,1024]{1,0:T(8,128)(2,1)S(1)} %add.7), channel_id=1, source_target_pairs={{0,16},{1,65},{2,18},{3,67},{4,20},{5,69},{6,22},{7,71},{8,56},{9,... | collective-permute-start | bytes 1572872 | tf_op jit(solution)/shard_map/ppermute | solution.py:272
  24.4 0.0 copy-done.1
  24.4 3.4 %encode_later.3 = (f32[256,1024]{1,0:T(8,128)S(1)}, f32[64,1024]{1,0:T(8,128)S(1)}, f32[64,1024]{1,0:T(8,128)S(1)}) custom-call(s32[8]{0:T(128)S(1)} %stack.35.place_ref, s32[2,512]{1,0:T(2,128)S(1)} %copy-done, bf16[8,2048]{1,0:T(8,128)(2,1)S(1)} %get-tuple-element.21.shots_ref, bf16[2048,1024]{1,0:T(8,128)(2,1)S(1)} %get-tuple-element.19.data_ref, ...), custom_call_target="tpu_custom_call" | custom-call | flops 1073741824 | bytes 8388608 | tf_op jit(solution)/shard_map/encode_later/pallas_call | solution.py:192
  27.8 0.0 collective-permute-done.back
  27.8 3.4 %collective-permute-done.2.near = bf16[256,1024]{1,0:T(8,128)(2,1)S(1)} collective-permute-done((bf16[256,1024]{1,0:T(8,128)(2,1)S(1)}, bf16[256,1024]{1,0:T(8,128)(2,1)S(1)}, u32[]{:S(2)}, u32[]{:S(2)}) %collective-permute-start.2) | collective-permute-done | bytes 524320 | tf_op jit(solution)/shard_map/ppermute | solution.py:272
  31.2 0.2 spread.1
  31.4 2.8 %collective-permute-start.3 = (bf16[64,1024]{1,0:T(8,128)(2,1)S(1)}, bf16[64,1024]{1,0:T(8,128)(2,1)S(1)}, u32[]{:S(2)}, u32[]{:S(2)}) collective-permute-start(bf16[64,1024]{1,0:T(8,128)(2,1)S(1)} %get-tuple-element.26), channel_id=1, source_target_pairs={{0,128},{1,33},{2,130},{3,35},{4,132},{5,37},{6,134},{7,39},{8,136... | collective-permute-start | bytes 393224 | tf_op jit(solution)/shard_map/ppermute | solution.py:272
  34.3 0.3 collective-permute-start.4
  34.6 2.4 %collective-permute-start.5 = (bf16[64,1024]{1,0:T(8,128)(2,1)S(1)}, bf16[64,1024]{1,0:T(8,128)(2,1)S(1)}, u32[]{:S(2)}, u32[]{:S(2)}) collective-permute-start(bf16[64,1024]{1,0:T(8,128)(2,1)S(1)} %get-tuple-element.28), channel_id=1, source_target_pairs={{0,192},{1,49},{2,194},{3,51},{4,196},{5,53},{6,198},{7,55},{8,72}... | collective-permute-start | bytes 393224 | tf_op jit(solution)/shard_map/ppermute | solution.py:272
  36.9 0.2 collective-permute-done.3.far
  37.1 2.2 %collective-permute-done.4.near = bf16[64,1024]{1,0:T(8,128)(2,1)S(1)} collective-permute-done((bf16[64,1024]{1,0:T(8,128)(2,1)S(1)}, bf16[64,1024]{1,0:T(8,128)(2,1)S(1)}, u32[]{:S(2)}, u32[]{:S(2)}) %collective-permute-start.4) | collective-permute-done | bytes 131104 | tf_op jit(solution)/shard_map/ppermute | solution.py:272
  39.3 0.0 collective-permute-done.5.back
  39.3 0.1 last.1
  39.4 0.1 reshape.7
  39.5 14.5 %all_to_all.18 = bf16[32,1,2,1024]{3,2,1,0:T(2,128)(2,1)S(1)} all-to-all(bf16[32,1,2,1024]{3,2,1,0:T(2,128)(2,1)S(1)} %bitcast.16), channel_id=1, replica_groups=mesh['z_hi'=4,'x'=4,'rcv'=16] {'rcv'}, dimensions={0} | all-to-all | bytes 262144 | tf_op jit(solution)/shard_map/all_to_all | solution.py:293
  54.0 0.7 %copy.7 = bf16[2,16,2,1024]{3,2,1,0:T(2,128)(2,1)} copy(bf16[2,16,2,1024]{3,2,0,1:T(2,128)(2,1)S(1)} %bitcast.17) | data formatting | bytes 262144 | tf_op jit(solution)/shard_map/all_to_all | solution.py:293
Async XLA Ops:
  0.0 8.3 %copy-start = (s32[2,512]{1,0:T(2,128)S(1)}, s32[2,512]{1,0:T(2,128)}, u32[]{:S(2)}) copy-start(s32[2,512]{1,0:T(2,128)} %ray_ref.5) | copy-start | bytes 12292
  4.4 13.5 %collective-permute-start.1 = (bf16[256,1024]{1,0:T(8,128)(2,1)S(1)}, bf16[256,1024]{1,0:T(8,128)(2,1)S(1)}, u32[]{:S(2)}, u32[]{:S(2)}) collective-permute-start(bf16[256,1024]{1,0:T(8,128)(2,1)S(1)} %get-tuple-element.24), channel_id=1, source_target_pairs={{0,16},{1,65},{2,18},{3,67},{4,20},{5,69},{6,22},{7,71},{8,56},{9,... | collective-permute-start | bytes 1572872 | tf_op jit(solution)/shard_map/ppermute | solution.py:272
  8.3 16.1 %copy-start.1 = (s32[2,1024]{1,0:T(2,128)S(1)}, s32[2,1024]{1,0:T(2,128)}, u32[]{:S(2)}) copy-start(s32[2,1024]{1,0:T(2,128)} %rcv_ref.1) | copy-start | bytes 24580
  12.8 15.0 %collective-permute-start = (bf16[256,1024]{1,0:T(8,128)(2,1)S(1)}, bf16[256,1024]{1,0:T(8,128)(2,1)S(1)}, u32[]{:S(2)}, u32[]{:S(2)}) collective-permute-start(bf16[256,1024]{1,0:T(8,128)(2,1)S(1)} %get-tuple-element.20), channel_id=1, source_target_pairs={{0,48},{1,193},{2,50},{3,195},{4,52},{5,197},{6,54},{7,199},{8,24}... | collective-permute-start | bytes 1572872 | tf_op jit(solution)/shard_map/ppermute | solution.py:272
  18.0 13.2 %collective-permute-start.2 = (bf16[256,1024]{1,0:T(8,128)(2,1)S(1)}, bf16[256,1024]{1,0:T(8,128)(2,1)S(1)}, u32[]{:S(2)}, u32[]{:S(2)}) collective-permute-start(bf16[256,1024]{1,0:T(8,128)(2,1)S(1)} %add.7), channel_id=1, source_target_pairs={{0,16},{1,65},{2,18},{3,67},{4,20},{5,69},{6,22},{7,71},{8,56},{9,... | collective-permute-start | bytes 1572872 | tf_op jit(solution)/shard_map/ppermute | solution.py:272
  31.4 5.7 %collective-permute-start.3 = (bf16[64,1024]{1,0:T(8,128)(2,1)S(1)}, bf16[64,1024]{1,0:T(8,128)(2,1)S(1)}, u32[]{:S(2)}, u32[]{:S(2)}) collective-permute-start(bf16[64,1024]{1,0:T(8,128)(2,1)S(1)} %get-tuple-element.26), channel_id=1, source_target_pairs={{0,128},{1,33},{2,130},{3,35},{4,132},{5,37},{6,134},{7,39},{8,136... | collective-permute-start | bytes 393224 | tf_op jit(solution)/shard_map/ppermute | solution.py:272
  34.3 5.0 %collective-permute-start.4 = (bf16[64,1024]{1,0:T(8,128)(2,1)S(1)}, bf16[64,1024]{1,0:T(8,128)(2,1)S(1)}, u32[]{:S(2)}, u32[]{:S(2)}) collective-permute-start(bf16[64,1024]{1,0:T(8,128)(2,1)S(1)} %get-tuple-element.27), channel_id=1, source_target_pairs={{0,64},{1,17},{2,66},{3,19},{4,68},{5,21},{6,70},{7,23},{8,200},{9... | collective-permute-start | bytes 393224 | tf_op jit(solution)/shard_map/ppermute | solution.py:272
  34.6 4.7 %collective-permute-start.5 = (bf16[64,1024]{1,0:T(8,128)(2,1)S(1)}, bf16[64,1024]{1,0:T(8,128)(2,1)S(1)}, u32[]{:S(2)}, u32[]{:S(2)}) collective-permute-start(bf16[64,1024]{1,0:T(8,128)(2,1)S(1)} %get-tuple-element.28), channel_id=1, source_target_pairs={{0,192},{1,49},{2,194},{3,51},{4,196},{5,53},{6,198},{7,55},{8,72}... | collective-permute-start | bytes 393224 | tf_op jit(solution)/shard_map/ppermute | solution.py:272

commit v5 on v4

--- a/solution.py
+++ b/solution.py
@@ -263,7 +263,7 @@
     pairs = []
     for index in range(ZH * XS * RCV):
         zh, x, rcv = index // (XS * RCV), index // RCV % XS, index % RCV
-        move = step[0] + step[1] * (1 - rcv // (RCV // 2) * 2)
+        move = step[0] + step[1] * (1 if rcv % CORES == 0 else 1 - rcv // (RCV // 2) * 2)
         if (rcv % CORES == 0) == (leg == 0):
             x = (x + move) % XS
         else:
@@ -275,7 +275,7 @@
 def on_device(spectra, shot_grid, ray_table, receiver_grid):
     zh, x, rcv = (lax.axis_index(name) for name in ("z_hi", "x", "rcv"))
     first_x = rcv % CORES == 0
-    turn = 1 - rcv // (RCV // 2) * 2
+    turn = jnp.where(first_x, 1, 1 - rcv // (RCV // 2) * 2)
     along_x, along_z = SHARE, RAYS // ZH
     spot = [zh, x, jnp.where(first_x, x, zh), BASE + rcv, turn]
     spot += [jnp.where(first_x, along_x, along_z), jnp.where(first_x, along_z, along_x), jnp.where(first_x, zh, x)]

time: 54.9 us -> 54.9 us (level)
  no operation moved by 1% of the time
where the time goes in v5:
time: 54.9 us; the launch traced here: 54.8 us
  starting transfers between devices  19 us (35%)
  blocking collectives  14.5 us (26%)
  Pallas kernels  12.6 us (23%)
  waiting for transfers between devices  7.76 us (14%)
  local copies, waits for them, and re-layouts  0.89 us (2%)
    ppermute x6, starting transfers between devices, send(): return lax.ppermute(value, ('z_hi', 'x', 'rcv'), pairs)  19 us
    all_to_all x1, blocking collectives, on_device(): lax.all_to_all(turned.reshape(SHARE, 1, 2, WIDTH), 'rcv', split_axis=0, c...  14.5 us
    pallas_call x2, Pallas kernels, later(): pl.pallas_call(own_kernel if more else functools.partial(later_kernel, st...  7.83 us
    ppermute x6, waiting for transfers between devices, send(): return lax.ppermute(value, ('z_hi', 'x', 'rcv'), pairs)  7.76 us
    pallas_call x1, Pallas kernels, first(): pl.pallas_call(first_kernel, out_shape=[jax.ShapeDtypeStruct((n, m), BF16...  4.34 us
  transfers between devices with their start and end apart: 6, of which 4 were waited for; matrix products, arithmetic and copies ran while one was open for 0% of the time, Pallas kernels for 14%

profile of v5, /device:TPU:1, one launch (start us, length us, event | category | flops | bytes accessed | tf_op | source)
XLA Modules:
  0.0 54.8 jit_solution(10552370901258518189)
XLA Ops:
  0.0 0.0 copy-start
  0.0 0.1 stack.35.place_ref
  0.1 4.3 %encode_first.1 = (bf16[256,1024]{1,0:T(8,128)(2,1)S(1)}, bf16[2048,1024]{1,0:T(8,128)(2,1)S(1)}, bf16[8,2048]{1,0:T(8,128)(2,1)S(1)}) custom-call(s32[8]{0:T(128)S(1)} %stack.35.place_ref, s32[2,512]{1,0:T(2,128)} %ray_ref.5, s32[2,1024]{1,0:T(2,128)} %grid_ref.1, bf16[1024,2,1024]{2,1,0:T(2,128)(2,1)} %bitcast.15), custom_call_target="tpu_custom_call" | custom-call | flops 1073741824 | bytes 8388608 | tf_op jit(solution)/shard_map/encode_first/pallas_call | solution.py:142
  4.4 3.9 %collective-permute-start.1 = (bf16[256,1024]{1,0:T(8,128)(2,1)S(1)}, bf16[256,1024]{1,0:T(8,128)(2,1)S(1)}, u32[]{:S(2)}, u32[]{:S(2)}) collective-permute-start(bf16[256,1024]{1,0:T(8,128)(2,1)S(1)} %get-tuple-element.24), channel_id=1, source_target_pairs={{0,16},{1,65},{2,18},{3,67},{4,20},{5,69},{6,22},{7,71},{8,24},{9,... | collective-permute-start | bytes 1572872 | tf_op jit(solution)/shard_map/ppermute | solution.py:272
  8.3 0.0 copy-done
  8.3 0.0 copy-start.1
  8.3 4.5 %encode_later.2 = (bf16[256,1024]{1,0:T(8,128)(2,1)S(1)}, f32[256,1024]{1,0:T(8,128)S(1)}) custom-call(s32[8]{0:T(128)S(1)} %stack.35.place_ref, s32[2,512]{1,0:T(2,128)S(1)} %copy-done, bf16[8,2048]{1,0:T(8,128)(2,1)S(1)} %get-tuple-element.21.shots_ref, bf16[2048,1024]{1,0:T(8,128)(2,1)S(1)} %get-tuple-element.19.data_ref), custom_call_target="tpu_custom_call" | custom-call | flops 2147483648 | bytes 8388608 | tf_op jit(solution)/shard_map/encode_later/pallas_call | solution.py:192
  12.8 3.1 %collective-permute-start = (bf16[256,1024]{1,0:T(8,128)(2,1)S(1)}, bf16[256,1024]{1,0:T(8,128)(2,1)S(1)}, u32[]{:S(2)}, u32[]{:S(2)}) collective-permute-start(bf16[256,1024]{1,0:T(8,128)(2,1)S(1)} %get-tuple-element.20), channel_id=1, source_target_pairs={{0,48},{1,193},{2,50},{3,195},{4,52},{5,197},{6,54},{7,199},{8,56}... | collective-permute-start | bytes 1572872 | tf_op jit(solution)/shard_map/ppermute | solution.py:272
  16.0 2.0 %collective-permute-done.1.refs_0_ = bf16[256,1024]{1,0:T(8,128)(2,1)S(1)} collective-permute-done((bf16[256,1024]{1,0:T(8,128)(2,1)S(1)}, bf16[256,1024]{1,0:T(8,128)(2,1)S(1)}, u32[]{:S(2)}, u32[]{:S(2)}) %collective-permute-start.1) | collective-permute-done | bytes 524320 | tf_op jit(solution)/shard_map/ppermute | solution.py:272
  17.9 0.1 add.7
  18.0 6.4 %collective-permute-start.2 = (bf16[256,1024]{1,0:T(8,128)(2,1)S(1)}, bf16[256,1024]{1,0:T(8,128)(2,1)S(1)}, u32[]{:S(2)}, u32[]{:S(2)}) collective-permute-start(bf16[256,1024]{1,0:T(8,128)(2,1)S(1)} %add.7), channel_id=1, source_target_pairs={{0,16},{1,65},{2,18},{3,67},{4,20},{5,69},{6,22},{7,71},{8,24},{9,... | collective-permute-start | bytes 1572872 | tf_op jit(solution)/shard_map/ppermute | solution.py:272
  24.4 0.0 copy-done.1
  24.4 3.4 %encode_later.3 = (f32[256,1024]{1,0:T(8,128)S(1)}, f32[64,1024]{1,0:T(8,128)S(1)}, f32[64,1024]{1,0:T(8,128)S(1)}) custom-call(s32[8]{0:T(128)S(1)} %stack.35.place_ref, s32[2,512]{1,0:T(2,128)S(1)} %copy-done, bf16[8,2048]{1,0:T(8,128)(2,1)S(1)} %get-tuple-element.21.shots_ref, bf16[2048,1024]{1,0:T(8,128)(2,1)S(1)} %get-tuple-element.19.data_ref, ...), custom_call_target="tpu_custom_call" | custom-call | flops 1073741824 | bytes 8388608 | tf_op jit(solution)/shard_map/encode_later/pallas_call | solution.py:192
  27.8 0.0 collective-permute-done.back
  27.8 3.4 %collective-permute-done.2.near = bf16[256,1024]{1,0:T(8,128)(2,1)S(1)} collective-permute-done((bf16[256,1024]{1,0:T(8,128)(2,1)S(1)}, bf16[256,1024]{1,0:T(8,128)(2,1)S(1)}, u32[]{:S(2)}, u32[]{:S(2)}) %collective-permute-start.2) | collective-permute-done | bytes 524320 | tf_op jit(solution)/shard_map/ppermute | solution.py:272
  31.2 0.2 spread.1
  31.4 2.8 %collective-permute-start.3 = (bf16[64,1024]{1,0:T(8,128)(2,1)S(1)}, bf16[64,1024]{1,0:T(8,128)(2,1)S(1)}, u32[]{:S(2)}, u32[]{:S(2)}) collective-permute-start(bf16[64,1024]{1,0:T(8,128)(2,1)S(1)} %get-tuple-element.26), channel_id=1, source_target_pairs={{0,128},{1,33},{2,130},{3,35},{4,132},{5,37},{6,134},{7,39},{8,136... | collective-permute-start | bytes 393224 | tf_op jit(solution)/shard_map/ppermute | solution.py:272
  34.3 0.3 collective-permute-start.4
  34.6 2.4 %collective-permute-start.5 = (bf16[64,1024]{1,0:T(8,128)(2,1)S(1)}, bf16[64,1024]{1,0:T(8,128)(2,1)S(1)}, u32[]{:S(2)}, u32[]{:S(2)}) collective-permute-start(bf16[64,1024]{1,0:T(8,128)(2,1)S(1)} %get-tuple-element.28), channel_id=1, source_target_pairs={{0,192},{1,49},{2,194},{3,51},{4,196},{5,53},{6,198},{7,55},{8,200... | collective-permute-start | bytes 393224 | tf_op jit(solution)/shard_map/ppermute | solution.py:272
  36.9 0.2 collective-permute-done.3.far
  37.1 2.2 %collective-permute-done.4.near = bf16[64,1024]{1,0:T(8,128)(2,1)S(1)} collective-permute-done((bf16[64,1024]{1,0:T(8,128)(2,1)S(1)}, bf16[64,1024]{1,0:T(8,128)(2,1)S(1)}, u32[]{:S(2)}, u32[]{:S(2)}) %collective-permute-start.4) | collective-permute-done | bytes 131104 | tf_op jit(solution)/shard_map/ppermute | solution.py:272
  39.3 0.0 collective-permute-done.5.back
  39.3 0.1 last.1
  39.4 0.1 reshape.7
  39.5 14.5 %all_to_all.18 = bf16[32,1,2,1024]{3,2,1,0:T(2,128)(2,1)S(1)} all-to-all(bf16[32,1,2,1024]{3,2,1,0:T(2,128)(2,1)S(1)} %bitcast.16), channel_id=1, replica_groups=mesh['z_hi'=4,'x'=4,'rcv'=16] {'rcv'}, dimensions={0} | all-to-all | bytes 262144 | tf_op jit(solution)/shard_map/all_to_all | solution.py:293
  54.0 0.7 %copy.7 = bf16[2,16,2,1024]{3,2,1,0:T(2,128)(2,1)} copy(bf16[2,16,2,1024]{3,2,0,1:T(2,128)(2,1)S(1)} %bitcast.17) | data formatting | bytes 262144 | tf_op jit(solution)/shard_map/all_to_all | solution.py:293
Async XLA Ops:
  0.0 8.3 %copy-start = (s32[2,512]{1,0:T(2,128)S(1)}, s32[2,512]{1,0:T(2,128)}, u32[]{:S(2)}) copy-start(s32[2,512]{1,0:T(2,128)} %ray_ref.5) | copy-start | bytes 12292
  4.4 13.5 %collective-permute-start.1 = (bf16[256,1024]{1,0:T(8,128)(2,1)S(1)}, bf16[256,1024]{1,0:T(8,128)(2,1)S(1)}, u32[]{:S(2)}, u32[]{:S(2)}) collective-permute-start(bf16[256,1024]{1,0:T(8,128)(2,1)S(1)} %get-tuple-element.24), channel_id=1, source_target_pairs={{0,16},{1,65},{2,18},{3,67},{4,20},{5,69},{6,22},{7,71},{8,24},{9,... | collective-permute-start | bytes 1572872 | tf_op jit(solution)/shard_map/ppermute | solution.py:272
  8.3 16.1 %copy-start.1 = (s32[2,1024]{1,0:T(2,128)S(1)}, s32[2,1024]{1,0:T(2,128)}, u32[]{:S(2)}) copy-start(s32[2,1024]{1,0:T(2,128)} %rcv_ref.1) | copy-start | bytes 24580
  12.8 15.0 %collective-permute-start = (bf16[256,1024]{1,0:T(8,128)(2,1)S(1)}, bf16[256,1024]{1,0:T(8,128)(2,1)S(1)}, u32[]{:S(2)}, u32[]{:S(2)}) collective-permute-start(bf16[256,1024]{1,0:T(8,128)(2,1)S(1)} %get-tuple-element.20), channel_id=1, source_target_pairs={{0,48},{1,193},{2,50},{3,195},{4,52},{5,197},{6,54},{7,199},{8,56}... | collective-permute-start | bytes 1572872 | tf_op jit(solution)/shard_map/ppermute | solution.py:272
  18.0 13.2 %collective-permute-start.2 = (bf16[256,1024]{1,0:T(8,128)(2,1)S(1)}, bf16[256,1024]{1,0:T(8,128)(2,1)S(1)}, u32[]{:S(2)}, u32[]{:S(2)}) collective-permute-start(bf16[256,1024]{1,0:T(8,128)(2,1)S(1)} %add.7), channel_id=1, source_target_pairs={{0,16},{1,65},{2,18},{3,67},{4,20},{5,69},{6,22},{7,71},{8,24},{9,... | collective-permute-start | bytes 1572872 | tf_op jit(solution)/shard_map/ppermute | solution.py:272
  31.4 5.7 %collective-permute-start.3 = (bf16[64,1024]{1,0:T(8,128)(2,1)S(1)}, bf16[64,1024]{1,0:T(8,128)(2,1)S(1)}, u32[]{:S(2)}, u32[]{:S(2)}) collective-permute-start(bf16[64,1024]{1,0:T(8,128)(2,1)S(1)} %get-tuple-element.26), channel_id=1, source_target_pairs={{0,128},{1,33},{2,130},{3,35},{4,132},{5,37},{6,134},{7,39},{8,136... | collective-permute-start | bytes 393224 | tf_op jit(solution)/shard_map/ppermute | solution.py:272
  34.3 5.0 %collective-permute-start.4 = (bf16[64,1024]{1,0:T(8,128)(2,1)S(1)}, bf16[64,1024]{1,0:T(8,128)(2,1)S(1)}, u32[]{:S(2)}, u32[]{:S(2)}) collective-permute-start(bf16[64,1024]{1,0:T(8,128)(2,1)S(1)} %get-tuple-element.27), channel_id=1, source_target_pairs={{0,64},{1,17},{2,66},{3,19},{4,68},{5,21},{6,70},{7,23},{8,72},{9,... | collective-permute-start | bytes 393224 | tf_op jit(solution)/shard_map/ppermute | solution.py:272
  34.6 4.7 %collective-permute-start.5 = (bf16[64,1024]{1,0:T(8,128)(2,1)S(1)}, bf16[64,1024]{1,0:T(8,128)(2,1)S(1)}, u32[]{:S(2)}, u32[]{:S(2)}) collective-permute-start(bf16[64,1024]{1,0:T(8,128)(2,1)S(1)} %get-tuple-element.28), channel_id=1, source_target_pairs={{0,192},{1,49},{2,194},{3,51},{4,196},{5,53},{6,198},{7,55},{8,200... | collective-permute-start | bytes 393224 | tf_op jit(solution)/shard_map/ppermute | solution.py:272

commit v6 on v5

--- a/solution.py
+++ b/solution.py
@@ -284,9 +284,10 @@
     relayed = send(far, 0, NEAR)
     back, near = later([BACK, NEAR], [BF16, F32], spot, ray_table, shots, data)
     from_back = send(back, 0, BACK)
-    from_near = send(add(near, relayed), 0, NEAR)
     shots, back = lax.optimization_barrier((shots, back))
     here, cosines, sines = later([HERE], [F32], spot, ray_table, shots, data, receiver_grid)
+    near, here = lax.optimization_barrier((near, here))
+    from_near = send(add(near, relayed), 0, NEAR)
     far, near, back, here = spread(here, from_back, from_near)
     pieces = [send(far, 1, FAR), send(near, 1, NEAR), send(back, 1, BACK)]
     turned = last(here, *pieces, cosines, sines)

time: 54.9 us -> 55.7 us (1.015)
  starting transfers between devices: 19 us -> 17.5 us
  waiting for transfers between devices: 7.76 us -> 9.16 us
  blocking collectives: 14.5 us -> 15.3 us
    ppermute x6, starting transfers between devices: 19 us -> 17.5 us  [send(): return lax.ppermute(value, ('z_hi', 'x', 'rcv'), pairs)]
    ppermute x6, waiting for transfers between devices: 7.76 us -> 9.16 us  [send(): return lax.ppermute(value, ('z_hi', 'x', 'rcv'), pairs)]
    all_to_all x1, blocking collectives: 14.5 us -> 15.3 us  [on_device(): lax.all_to_all(turned.reshape(SHARE, 1, 2, WIDTH), 'rcv', split_axis=0, c...]
  transfers between devices with their start and end apart: 6 -> 6, of which waited for: 4 -> 3; matrix products, arithmetic and copies ran while one was open for 0% -> 0% of each run, Pallas kernels for 14% -> 14%
where the time goes in v6:
time: 55.7 us; the launch traced here: 55.5 us
  starting transfers between devices  17.5 us (31%)
  blocking collectives  15.3 us (27%)
  Pallas kernels  12.6 us (23%)
  waiting for transfers between devices  9.16 us (16%)
  local copies, waits for them, and re-layouts  0.89 us (2%)
    ppermute x6, starting transfers between devices, send(): return lax.ppermute(value, ('z_hi', 'x', 'rcv'), pairs)  17.5 us
    all_to_all x1, blocking collectives, on_device(): lax.all_to_all(turned.reshape(SHARE, 1, 2, WIDTH), 'rcv', split_axis=0, c...  15.3 us
    ppermute x6, waiting for transfers between devices, send(): return lax.ppermute(value, ('z_hi', 'x', 'rcv'), pairs)  9.16 us
    pallas_call x2, Pallas kernels, later(): pl.pallas_call(own_kernel if more else functools.partial(later_kernel, st...  7.84 us
    pallas_call x1, Pallas kernels, first(): pl.pallas_call(first_kernel, out_shape=[jax.ShapeDtypeStruct((n, m), BF16...  4.34 us
  transfers between devices with their start and end apart: 6, of which 3 were waited for; matrix products, arithmetic and copies ran while one was open for 0% of the time, Pallas kernels for 14%

profile of v6, /device:TPU:1, one launch (start us, length us, event | category | flops | bytes accessed | tf_op | source)
XLA Modules:
  0.0 55.5 jit_solution(16019046609042393268)
XLA Ops:
  0.0 0.0 copy-start
  0.0 0.1 stack.35.place_ref
  0.1 4.3 %encode_first.1 = (bf16[256,1024]{1,0:T(8,128)(2,1)S(1)}, bf16[2048,1024]{1,0:T(8,128)(2,1)S(1)}, bf16[8,2048]{1,0:T(8,128)(2,1)S(1)}) custom-call(s32[8]{0:T(128)S(1)} %stack.35.place_ref, s32[2,512]{1,0:T(2,128)} %ray_ref.5, s32[2,1024]{1,0:T(2,128)} %grid_ref.1, bf16[1024,2,1024]{2,1,0:T(2,128)(2,1)} %bitcast.15), custom_call_target="tpu_custom_call" | custom-call | flops 1073741824 | bytes 8388608 | tf_op jit(solution)/shard_map/encode_first/pallas_call | solution.py:142
  4.4 0.0 copy-start.1
  4.5 3.9 %collective-permute-start.1 = (bf16[256,1024]{1,0:T(8,128)(2,1)S(1)}, bf16[256,1024]{1,0:T(8,128)(2,1)S(1)}, u32[]{:S(2)}, u32[]{:S(2)}) collective-permute-start(bf16[256,1024]{1,0:T(8,128)(2,1)S(1)} %get-tuple-element.28), channel_id=1, source_target_pairs={{0,16},{1,65},{2,18},{3,67},{4,20},{5,69},{6,22},{7,71},{8,24},{9,... | collective-permute-start | bytes 1572872 | tf_op jit(solution)/shard_map/ppermute | solution.py:272
  8.3 0.0 copy-done
  8.4 4.5 %encode_later.2 = (bf16[256,1024]{1,0:T(8,128)(2,1)S(1)}, f32[256,1024]{1,0:T(8,128)S(1)}) custom-call(s32[8]{0:T(128)S(1)} %stack.35.place_ref, s32[2,512]{1,0:T(2,128)S(1)} %copy-done, bf16[8,2048]{1,0:T(8,128)(2,1)S(1)} %get-tuple-element.24.shots_ref, bf16[2048,1024]{1,0:T(8,128)(2,1)S(1)} %get-tuple-element.21.data_ref), custom_call_target="tpu_custom_call" | custom-call | flops 2147483648 | bytes 8388608 | tf_op jit(solution)/shard_map/encode_later/pallas_call | solution.py:192
  12.8 3.1 %collective-permute-start = (bf16[256,1024]{1,0:T(8,128)(2,1)S(1)}, bf16[256,1024]{1,0:T(8,128)(2,1)S(1)}, u32[]{:S(2)}, u32[]{:S(2)}) collective-permute-start(bf16[256,1024]{1,0:T(8,128)(2,1)S(1)} %get-tuple-element.23), channel_id=1, source_target_pairs={{0,48},{1,193},{2,50},{3,195},{4,52},{5,197},{6,54},{7,199},{8,56}... | collective-permute-start | bytes 1572872 | tf_op jit(solution)/shard_map/ppermute | solution.py:272
  16.0 0.0 copy-done.1
  16.0 3.4 %encode_later.3 = (f32[256,1024]{1,0:T(8,128)S(1)}, f32[64,1024]{1,0:T(8,128)S(1)}, f32[64,1024]{1,0:T(8,128)S(1)}) custom-call(s32[8]{0:T(128)S(1)} %stack.35.place_ref, s32[2,512]{1,0:T(2,128)S(1)} %copy-done, bf16[8,2048]{1,0:T(8,128)(2,1)S(1)} %get-tuple-element.24.shots_ref, bf16[2048,1024]{1,0:T(8,128)(2,1)S(1)} %get-tuple-element.21.data_ref, ...), custom_call_target="tpu_custom_call" | custom-call | flops 1073741824 | bytes 8388608 | tf_op jit(solution)/shard_map/encode_later/pallas_call | solution.py:192
  19.3 0.0 collective-permute-done.1.refs_0_
  19.3 0.1 add.7
  19.4 5.0 %collective-permute-start.2 = (bf16[256,1024]{1,0:T(8,128)(2,1)S(1)}, bf16[256,1024]{1,0:T(8,128)(2,1)S(1)}, u32[]{:S(2)}, u32[]{:S(2)}) collective-permute-start(bf16[256,1024]{1,0:T(8,128)(2,1)S(1)} %add.7), channel_id=1, source_target_pairs={{0,16},{1,65},{2,18},{3,67},{4,20},{5,69},{6,22},{7,71},{8,24},{9,... | collective-permute-start | bytes 1572872 | tf_op jit(solution)/shard_map/ppermute | solution.py:272
  24.5 0.0 collective-permute-done.back
  24.5 6.8 %collective-permute-done.2.near = bf16[256,1024]{1,0:T(8,128)(2,1)S(1)} collective-permute-done((bf16[256,1024]{1,0:T(8,128)(2,1)S(1)}, bf16[256,1024]{1,0:T(8,128)(2,1)S(1)}, u32[]{:S(2)}, u32[]{:S(2)}) %collective-permute-start.2) | collective-permute-done | bytes 524320 | tf_op jit(solution)/shard_map/ppermute | solution.py:272
  31.3 0.2 spread.1
  31.4 2.8 %collective-permute-start.3 = (bf16[64,1024]{1,0:T(8,128)(2,1)S(1)}, bf16[64,1024]{1,0:T(8,128)(2,1)S(1)}, u32[]{:S(2)}, u32[]{:S(2)}) collective-permute-start(bf16[64,1024]{1,0:T(8,128)(2,1)S(1)} %get-tuple-element.30), channel_id=1, source_target_pairs={{0,128},{1,33},{2,130},{3,35},{4,132},{5,37},{6,134},{7,39},{8,136... | collective-permute-start | bytes 393224 | tf_op jit(solution)/shard_map/ppermute | solution.py:272
  34.3 0.3 collective-permute-start.4
  34.6 2.4 %collective-permute-start.5 = (bf16[64,1024]{1,0:T(8,128)(2,1)S(1)}, bf16[64,1024]{1,0:T(8,128)(2,1)S(1)}, u32[]{:S(2)}, u32[]{:S(2)}) collective-permute-start(bf16[64,1024]{1,0:T(8,128)(2,1)S(1)} %get-tuple-element.32), channel_id=1, source_target_pairs={{0,192},{1,49},{2,194},{3,51},{4,196},{5,53},{6,198},{7,55},{8,200... | collective-permute-start | bytes 393224 | tf_op jit(solution)/shard_map/ppermute | solution.py:272
  36.9 0.2 collective-permute-done.3.far
  37.1 2.2 %collective-permute-done.4.near = bf16[64,1024]{1,0:T(8,128)(2,1)S(1)} collective-permute-done((bf16[64,1024]{1,0:T(8,128)(2,1)S(1)}, bf16[64,1024]{1,0:T(8,128)(2,1)S(1)}, u32[]{:S(2)}, u32[]{:S(2)}) %collective-permute-start.4) | collective-permute-done | bytes 131104 | tf_op jit(solution)/shard_map/ppermute | solution.py:272
  39.3 0.0 collective-permute-done.5.back
  39.3 0.1 last.1
  39.4 0.1 reshape.7
  39.5 15.3 %all_to_all.18 = bf16[32,1,2,1024]{3,2,1,0:T(2,128)(2,1)S(1)} all-to-all(bf16[32,1,2,1024]{3,2,1,0:T(2,128)(2,1)S(1)} %bitcast.16), channel_id=1, replica_groups=mesh['z_hi'=4,'x'=4,'rcv'=16] {'rcv'}, dimensions={0} | all-to-all | bytes 262144 | tf_op jit(solution)/shard_map/all_to_all | solution.py:294
  54.8 0.7 %copy.7 = bf16[2,16,2,1024]{3,2,1,0:T(2,128)(2,1)} copy(bf16[2,16,2,1024]{3,2,0,1:T(2,128)(2,1)S(1)} %bitcast.17) | data formatting | bytes 262144 | tf_op jit(solution)/shard_map/all_to_all | solution.py:294
Async XLA Ops:
  0.0 8.4 %copy-start = (s32[2,512]{1,0:T(2,128)S(1)}, s32[2,512]{1,0:T(2,128)}, u32[]{:S(2)}) copy-start(s32[2,512]{1,0:T(2,128)} %ray_ref.5) | copy-start | bytes 12292
  4.4 11.5 %copy-start.1 = (s32[2,1024]{1,0:T(2,128)S(1)}, s32[2,1024]{1,0:T(2,128)}, u32[]{:S(2)}) copy-start(s32[2,1024]{1,0:T(2,128)} %rcv_ref.1) | copy-start | bytes 24580
  4.5 14.9 %collective-permute-start.1 = (bf16[256,1024]{1,0:T(8,128)(2,1)S(1)}, bf16[256,1024]{1,0:T(8,128)(2,1)S(1)}, u32[]{:S(2)}, u32[]{:S(2)}) collective-permute-start(bf16[256,1024]{1,0:T(8,128)(2,1)S(1)} %get-tuple-element.28), channel_id=1, source_target_pairs={{0,16},{1,65},{2,18},{3,67},{4,20},{5,69},{6,22},{7,71},{8,24},{9,... | collective-permute-start | bytes 1572872 | tf_op jit(solution)/shard_map/ppermute | solution.py:272
  12.8 11.6 %collective-permute-start = (bf16[256,1024]{1,0:T(8,128)(2,1)S(1)}, bf16[256,1024]{1,0:T(8,128)(2,1)S(1)}, u32[]{:S(2)}, u32[]{:S(2)}) collective-permute-start(bf16[256,1024]{1,0:T(8,128)(2,1)S(1)} %get-tuple-element.23), channel_id=1, source_target_pairs={{0,48},{1,193},{2,50},{3,195},{4,52},{5,197},{6,54},{7,199},{8,56}... | collective-permute-start | bytes 1572872 | tf_op jit(solution)/shard_map/ppermute | solution.py:272
  19.4 11.8 %collective-permute-start.2 = (bf16[256,1024]{1,0:T(8,128)(2,1)S(1)}, bf16[256,1024]{1,0:T(8,128)(2,1)S(1)}, u32[]{:S(2)}, u32[]{:S(2)}) collective-permute-start(bf16[256,1024]{1,0:T(8,128)(2,1)S(1)} %add.7), channel_id=1, source_target_pairs={{0,16},{1,65},{2,18},{3,67},{4,20},{5,69},{6,22},{7,71},{8,24},{9,... | collective-permute-start | bytes 1572872 | tf_op jit(solution)/shard_map/ppermute | solution.py:272
  31.4 5.7 %collective-permute-start.3 = (bf16[64,1024]{1,0:T(8,128)(2,1)S(1)}, bf16[64,1024]{1,0:T(8,128)(2,1)S(1)}, u32[]{:S(2)}, u32[]{:S(2)}) collective-permute-start(bf16[64,1024]{1,0:T(8,128)(2,1)S(1)} %get-tuple-element.30), channel_id=1, source_target_pairs={{0,128},{1,33},{2,130},{3,35},{4,132},{5,37},{6,134},{7,39},{8,136... | collective-permute-start | bytes 393224 | tf_op jit(solution)/shard_map/ppermute | solution.py:272
  34.3 5.0 %collective-permute-start.4 = (bf16[64,1024]{1,0:T(8,128)(2,1)S(1)}, bf16[64,1024]{1,0:T(8,128)(2,1)S(1)}, u32[]{:S(2)}, u32[]{:S(2)}) collective-permute-start(bf16[64,1024]{1,0:T(8,128)(2,1)S(1)} %get-tuple-element.31), channel_id=1, source_target_pairs={{0,64},{1,17},{2,66},{3,19},{4,68},{5,21},{6,70},{7,23},{8,72},{9,... | collective-permute-start | bytes 393224 | tf_op jit(solution)/shard_map/ppermute | solution.py:272
  34.6 4.7 %collective-permute-start.5 = (bf16[64,1024]{1,0:T(8,128)(2,1)S(1)}, bf16[64,1024]{1,0:T(8,128)(2,1)S(1)}, u32[]{:S(2)}, u32[]{:S(2)}) collective-permute-start(bf16[64,1024]{1,0:T(8,128)(2,1)S(1)} %get-tuple-element.32), channel_id=1, source_target_pairs={{0,192},{1,49},{2,194},{3,51},{4,196},{5,53},{6,198},{7,55},{8,200... | collective-permute-start | bytes 393224 | tf_op jit(solution)/shard_map/ppermute | solution.py:272
